TPU v7x, 256 devices: a whole 4x4x8 slice. The times are simulated.
256 devices in a mesh: row: 8 (over z_hi, y), col: 8 (over z_lo, core), depth: 4 (over x).
Axes of the slice: x: 4, y: 4, z: 8 (z_hi: 2, z_lo: 4; z = z_hi * 4 + z_lo), core: 2. Of those that a mesh axis runs over, the one named last changes fastest.
Arguments:
- inputs: bfloat16 [512, 14848], P(('depth', 'row'), 'col'), may hold values from -0.59765625 to 0.59765625
- preact: bfloat16 [512, 16384], P(('depth', 'col'), 'row'), may hold values from -6 to 6
- grad_out: bfloat16 [512, 14848], P(('depth', 'row'), 'col'), may hold values from -1.796875 to 1.796875
- w_in: bfloat16 [16384, 14848], P(('row', 'depth'), 'col'), may hold values from -0.046875 to 0.046875
- w_out: bfloat16 [14848, 16384], P(('col', 'depth'), 'row'), may hold values from -0.046875 to 0.046875
Outputs:
- grad_in: bfloat16 [512, 14848], P(('depth', 'row'), 'col')
- grad_w_in: bfloat16 [16384, 14848], P(('row', 'depth'), 'col')
- grad_w_out: bfloat16 [14848, 16384], P(('col', 'depth'), 'row')
All inputs are finite; a program needn't handle non-finite values.
Results may differ from a plain program's by a relative error of at most 0.025.
Values may be sent and summed in bfloat16 or wider, within the bound.
No kernel may reach another device: no remote copies, remote signals or barrier semaphores. Data moves between devices by JAX's collectives and lax.ppermute only.
A program may use at most 64 MiB of HBM per device.

v0:
```python
import jax
import jax.numpy as jnp
from jax import lax
from jax.experimental.layout import Layout, with_layout_constraint
from jax.sharding import Mesh, PartitionSpec as P

AXES = ("zh", "y", "zl", "core", "xa", "xb")
ZH, Y, ZL, CORE, XA, XB = 2, 4, 4, 2, 2, 2
X = XA * XB
DEPTH = ("xa", "xb")
ROWS = Layout(major_to_minor=(0, 1))


def flip(value, axes, bits, size):
    return lax.ppermute(value, axes, [(i, i ^ bits) for i in range(size)])


def dot(left, right):
    return jnp.dot(left, right, preferred_element_type=jnp.float32)


def wide(value):
    return value.astype(jnp.float32)


def over_tokens(left, right):
    return lax.dot_general(
        left, right, (((0,), (0,)), ((), ())), preferred_element_type=jnp.float32
    )


def exchange(blocks, axes):
    return lax.all_to_all(blocks, axes, 0, 0, tiled=True)


def added(blocks):
    return jnp.sum(wide(blocks), axis=0)


def ordered(mine, other, index):
    first = jnp.where(index == 0, mine, other)
    second = jnp.where(index == 0, other, mine)
    return jnp.stack([first, second])


def beside(*transfers):
    return lax.optimization_barrier(transfers)


def after(value, other):
    return lax.optimization_barrier((value, other))[0]


def pick(blocks, index):
    return lax.dynamic_index_in_dim(blocks, index, 0, keepdims=False)


def relative(blocks, index):
    return jnp.stack([pick(blocks, index ^ k) for k in range(blocks.shape[0])])


def plus(mine, others):
    return sum((wide(other) for other in others), wide(mine))


def body(inputs, preact, grad_out, w_in, w_out):
    zh, y, zl = lax.axis_index("zh"), lax.axis_index("y"), lax.axis_index("zl")
    core, x = lax.axis_index("core"), lax.axis_index(DEPTH)
    rows, feats = grad_out.shape
    hid = preact.shape[1]
    part = feats // X
    hid_part = hid // X

    def over_x(value, k):
        return flip(value, DEPTH, k, X)

    def over_y(value, k):
        return flip(value, "y", k, Y)

    pre_value = wide(preact)
    normal_cdf = 0.5 * (1.0 + jax.scipy.special.erf(pre_value * 0.7071067811865476))
    density = jnp.exp(-0.5 * pre_value * pre_value) * 0.3989422804014327
    slope = normal_cdf + pre_value * density
    act = (pre_value * normal_cdf).astype(jnp.bfloat16)
    slope, act = lax.optimization_barrier((slope, act))

    dy = ordered(grad_out, flip(grad_out, "zh", 1, ZH), zh)
    act_send = after(act, dy)
    x_pair = jnp.stack([inputs, flip(inputs, "zh", 1, ZH)])

    dy = dy.reshape(ZH, rows, X, part).transpose(2, 0, 1, 3)
    dy = jnp.broadcast_to(dy, (Y,) + dy.shape).reshape(Y * X, ZH * rows, part)
    dy, x_far, act_far = beside(
        exchange(dy, ("y",) + DEPTH),
        [over_x(x_pair, k) for k in (1, 2, 3)],
        [flip(act_send, "zl", k, ZL) for k in (1, 2, 3)],
    )
    x_rows = jnp.stack([x_pair] + x_far).reshape(-1, feats)
    act = jnp.concatenate([act] + act_far)
    dy = dy.reshape(Y // 2, 2, X, ZH, rows, part)
    dy = dy.transpose(1, 2, 3, 0, 4, 5).reshape(CORE, X, ZL * rows, part)

    dy_x = relative(dy.transpose(1, 0, 2, 3), x).transpose(1, 0, 2, 3)
    dy_x = dy_x.reshape(CORE, X * ZL * rows, part)
    theirs = dot(pick(dy_x, 1 - core), w_out).astype(jnp.bfloat16)
    sums = dot(pick(dy_x, core), w_out) + wide(flip(theirs, "core", 1, CORE))
    sums = sums.astype(jnp.bfloat16).reshape(X, ZL * rows, hid)
    sums, x_rows = lax.optimization_barrier((sums, x_rows))

    y_rows = after(x_rows, sums)
    others, x_one, x_three = beside(
        [over_x(sums[k], k) for k in (1, 2, 3)], over_y(y_rows, 1), over_y(y_rows, 3)
    )
    sums = plus(sums[0], others).astype(jnp.bfloat16).reshape(ZL, rows, hid)

    send = after(act, sums)
    act_grad, act_one, act_three = beside(
        exchange(sums, ("zl",)), over_x(send, 1), over_x(send, 3)
    )

    hid_grad = (added(act_grad) * slope).astype(jnp.bfloat16)
    dz = hid_grad.reshape(rows, X, 1, hid_part).transpose(1, 2, 0, 3)
    dz = jnp.broadcast_to(dz, (X, ZL, rows, hid_part)).reshape(X * ZL, rows, hid_part)
    dz, x_two, act_two = beside(
        exchange(dz, DEPTH + ("zl",)),
        over_y(after(x_rows, dz), 2),
        over_x(after(act, dz), 2),
    )
    dz = ordered(dz, flip(dz, "core", 1, CORE), core)
    dz = dz.reshape(CORE, X, ZH, Y // 2, rows, hid_part)
    dz = dz.transpose(3, 0, 1, 2, 4, 5).reshape(Y, X, ZH, rows, hid_part)
    dz = relative(relative(dz, y).transpose(1, 0, 2, 3, 4), x).transpose(2, 0, 1, 3, 4)
    own, far = pick(dz, zh), pick(dz, 1 - zh).transpose(1, 0, 2, 3)
    dz = jnp.stack([own, far]).reshape(-1, hid_part)

    total = with_layout_constraint(dot(dz, w_in).astype(jnp.bfloat16), ROWS)
    total = total.reshape(2, 4, 4 * rows, feats)

    dz = jnp.stack([own.transpose(1, 0, 2, 3), far], 2).reshape(-1, hid_part)
    x_rows = jnp.concatenate([x_rows, x_one, x_two, x_three])
    grad_w_in = over_tokens(dz, x_rows).astype(jnp.bfloat16)

    act = jnp.concatenate([act, act_one, act_two, act_three])
    act_far = flip(act, "core", 1, CORE)

    own, far = beside(
        [over_x(total[0, k], k) for k in (1, 2, 3)],
        [over_y(total[1, k], k) for k in (1, 2, 3)],
    )
    own = plus(total[0, 0], own).astype(jnp.bfloat16).reshape(4, rows, feats)
    far = plus(total[1, 0], far).astype(jnp.bfloat16).reshape(4, rows, feats)
    rest = beside(
        [over_y(own[k], k) for k in (1, 2, 3)], [over_x(far[k], k) for k in (1, 2, 3)]
    )
    rest, act, act_far = beside(rest, act, act_far)
    (own_rest, far_rest), grad_w_in = beside(rest, grad_w_in)
    far = flip(plus(far[0], far_rest).astype(jnp.bfloat16), "zh", 1, ZH)
    grad_in = (plus(own[0], own_rest) + wide(far)).astype(jnp.bfloat16)

    dy = dy.reshape(CORE, X, ZL, rows, part).transpose(1, 2, 0, 3, 4)
    dy = relative(relative(dy, x).transpose(1, 0, 2, 3, 4), zl).transpose(2, 1, 0, 3, 4)
    grad_w_out = over_tokens(pick(dy, core).reshape(-1, part), act)
    grad_w_out = grad_w_out + over_tokens(pick(dy, 1 - core).reshape(-1, part), act_far)
    return (grad_in, grad_w_in, grad_w_out.astype(jnp.bfloat16))


def solution(mesh):
    fine = Mesh(mesh.devices.reshape(ZH, Y, ZL, CORE, XA, XB), AXES)
    row, col = ("zh", "y"), ("zl", "core")
    return jax.shard_map(
        body,
        mesh=fine,
        in_specs=(
            P(DEPTH + row, col),
            P(DEPTH + col, row),
            P(DEPTH + row, col),
            P(row + DEPTH, col),
            P(col + DEPTH, row),
        ),
        out_specs=(
            P(DEPTH + row, col),
            P(row + DEPTH, col),
            P(col + DEPTH, row),
        ),
        check_vma=False,
    )
```

profile of v0, /device:TPU:8, one launch (start us, length us, event | category | flops | bytes accessed | tf_op | source)
XLA Modules:
  0.0 143.2 jit_solution(8258272560050811051)
XLA Ops:
  0.7 7.3 %collective-permute-start = (bf16[16,1856]{1,0:T(8,128)(2,1)}, bf16[16,1856]{1,0:T(8,128)(2,1)S(1)}, u32[]{:S(2)}, u32[]{:S(2)}) collective-permute-start(bf16[16,1856]{1,0:T(8,128)(2,1)} %param.7), channel_id=1, source_target_pairs={{0,128},{128,0},{1,129},{129,1},{2,130},{130,2},{3,131},{131,3},{4... | collective-permute-start | bytes 178184 | tf_op jit(solution)/shard_map/ppermute | solution.py:15
  8.0 2.8 %collective-permute-done = bf16[16,1856]{1,0:T(8,128)(2,1)S(1)} collective-permute-done((bf16[16,1856]{1,0:T(8,128)(2,1)}, bf16[16,1856]{1,0:T(8,128)(2,1)S(1)}, u32[]{:S(2)}, u32[]{:S(2)}) %collective-permute-start) | collective-permute-done | bytes 59424 | tf_op jit(solution)/shard_map/ppermute | solution.py:15
  10.8 0.8 broadcast_select_fusion.3
  12.1 0.9 broadcast_in_dim.10
  13.0 7.4 %all-to-all-start = ((bf16[16,32,464]{2,1,0:T(8,128)(2,1)}), bf16[16,32,464]{2,1,0:T(8,128)(2,1)S(1)}, u32[]{:S(2)}, u32[]{:S(2)}) async-start(bf16[16,32,464]{2,1,0:T(8,128)(2,1)} %bitcast.1), calls=%async_computation | async-start | bytes 1048576 | tf_op jit(solution)/shard_map/all_to_all | solution.py:33
  20.4 3.0 %collective-permute-start.7 = (bf16[16,2048]{1,0:T(8,128)(2,1)S(1)}, bf16[16,2048]{1,0:T(8,128)(2,1)S(1)}, u32[]{:S(2)}, u32[]{:S(2)}) collective-permute-start(bf16[16,2048]{1,0:T(8,128)(2,1)S(1)} %get-tuple-element.56), channel_id=1, source_target_pairs={{0,24},{8,16},{16,8},{24,0},{1,25},{9,17},{17,9},{25,1},{2,26},{10... | collective-permute-start | bytes 196616 | tf_op jit(solution)/shard_map/ppermute | solution.py:15
  23.4 2.8 %collective-permute-start.4 = (bf16[2,16,1856]{2,1,0:T(8,128)(2,1)S(1)}, bf16[2,16,1856]{2,1,0:T(8,128)(2,1)S(1)}, u32[]{:S(2)}, u32[]{:S(2)}) collective-permute-start(bf16[2,16,1856]{2,1,0:T(8,128)(2,1)S(1)} %get-tuple-element.156), channel_id=1, source_target_pairs={{0,3},{1,2},{2,1},{3,0},{4,7},{5,6},{6,5},{7,4},{8,11},{9,10},{10,... | collective-permute-start | bytes 356360 | tf_op jit(solution)/shard_map/ppermute | solution.py:15
  26.2 0.9 collective-permute-start.3
  27.1 0.6 collective-permute-start.2
  27.6 1.6 %collective-permute-start.6 = (bf16[16,2048]{1,0:T(8,128)(2,1)S(1)}, bf16[16,2048]{1,0:T(8,128)(2,1)S(1)}, u32[]{:S(2)}, u32[]{:S(2)}) collective-permute-start(bf16[16,2048]{1,0:T(8,128)(2,1)S(1)} %get-tuple-element.56), channel_id=1, source_target_pairs={{0,16},{8,24},{16,0},{24,8},{1,17},{9,25},{17,1},{25,9},{2,18},{10... | collective-permute-start | bytes 196616 | tf_op jit(solution)/shard_map/ppermute | solution.py:15
  29.3 3.5 %collective-permute-done.6 = bf16[16,2048]{1,0:T(8,128)(2,1)S(1)} collective-permute-done((bf16[16,2048]{1,0:T(8,128)(2,1)S(1)}, bf16[16,2048]{1,0:T(8,128)(2,1)S(1)}, u32[]{:S(2)}, u32[]{:S(2)}) %collective-permute-start.6) | collective-permute-done | bytes 65568 | tf_op jit(solution)/shard_map/ppermute | solution.py:15
  32.8 0.7 collective-permute-done.5
  33.6 0.6 copy-done.10
  34.3 1.7 %convolution_convert_fusion.2 = bf16[256,2048]{1,0:T(8,128)(2,1)} fusion(bf16[464,2048]{1,0:T(8,128)(2,1)S(1)} %copy-done, bf16[2,256,464]{2,1,0:T(8,128)(2,1)S(1)} %bitcast.142, s32[]{:T(128)S(6)} %select_n.97), kind=kOutput, calls=%fused_computation.3 | convolution fusion | flops 487063552 | bytes 3211268 | tf_op jit(solution)/shard_map/dot_general | solution.py:19
  36.0 0.6 constant_dynamic-update-slice_fusion.10
  36.6 1.0 pad_maximum_fusion.7
  37.7 1.3 collective-permute-done.8
  39.0 1.9 %add_convert_fusion.1 = bf16[256,2048]{1,0:T(8,128)(2,1)S(1)} fusion(bf16[256,2048]{1,0:T(8,128)(2,1)} %collective-permute-done.8, bf16[464,2048]{1,0:T(8,128)(2,1)S(1)} %copy-done, bf16[2,256,464]{2,1,0:T(8,128)(2,1)S(1)} %bitcast.143, s32[]{:T(128)S(6)} %select_n.96), kind=kOutput, calls=%fused_computation.4 | convolution fusion | flops 488112128 | bytes 4259844 | tf_op jit(solution)/shard_map/dot_general | solution.py:19
  41.0 1.6 %collective-permute-start.13 = (bf16[128,1856]{1,0:T(8,128)(2,1)S(1)}, bf16[128,1856]{1,0:T(8,128)(2,1)S(1)}, u32[]{:S(2)}, u32[]{:S(2)}) collective-permute-start(bf16[128,1856]{1,0:T(8,128)(2,1)S(1)} %bitcast.152), channel_id=1, source_target_pairs={{0,96},{32,64},{64,32},{96,0},{1,97},{33,65},{65,33},{97,1},{2,98}... | collective-permute-start | bytes 1425416 | tf_op jit(solution)/shard_map/ppermute | solution.py:15
  42.5 1.8 %collective-permute-start.12 = (bf16[128,1856]{1,0:T(8,128)(2,1)S(1)}, bf16[128,1856]{1,0:T(8,128)(2,1)S(1)}, u32[]{:S(2)}, u32[]{:S(2)}) collective-permute-start(bf16[128,1856]{1,0:T(8,128)(2,1)S(1)} %bitcast.153), channel_id=1, source_target_pairs={{0,32},{32,0},{64,96},{96,64},{1,33},{33,1},{65,97},{97,65},{2,34}... | collective-permute-start | bytes 1425416 | tf_op jit(solution)/shard_map/ppermute | solution.py:15
  44.4 2.8 %collective-permute-start.11 = (bf16[64,2048]{1,0:T(8,128)(2,1)S(1)}, bf16[64,2048]{1,0:T(8,128)(2,1)S(1)}, u32[]{:S(2)}, u32[]{:S(2)}) collective-permute-start(bf16[64,2048]{1,0:T(8,128)(2,1)S(1)} %get-tuple-element.117), channel_id=1, source_target_pairs={{0,3},{1,2},{2,1},{3,0},{4,7},{5,6},{6,5},{7,4},{8,11},{9,10},{10,... | collective-permute-start | bytes 786440 | tf_op jit(solution)/shard_map/ppermute | solution.py:15
  47.1 0.9 collective-permute-start.10
  48.5 0.6 constant_dynamic-update-slice_fusion.9
  49.2 0.6 constant_dynamic-update-slice_fusion.8
  49.8 9.2 %collective-permute-done.11 = bf16[64,2048]{1,0:T(8,128)(2,1)S(1)} collective-permute-done((bf16[64,2048]{1,0:T(8,128)(2,1)S(1)}, bf16[64,2048]{1,0:T(8,128)(2,1)S(1)}, u32[]{:S(2)}, u32[]{:S(2)}) %collective-permute-start.11) | collective-permute-done | bytes 262176 | tf_op jit(solution)/shard_map/ppermute | solution.py:15
  59.1 0.6 collective-permute-done.9
  59.7 1.0 fusion.9
  60.8 3.4 %all-to-all-start.1 = ((bf16[4,16,2048]{2,1,0:T(8,128)(2,1)}), bf16[4,16,2048]{2,1,0:T(8,128)(2,1)S(1)}, u32[]{:S(2)}, u32[]{:S(2)}) async-start(bf16[4,16,2048]{2,1,0:T(8,128)(2,1)} %bitcast.26), calls=%async_computation.1 | async-start | bytes 524288 | tf_op jit(solution)/shard_map/all_to_all | solution.py:33
  64.2 0.7 constant_dynamic-update-slice_fusion.7
  64.8 2.7 %collective-permute-start.15 = (bf16[64,2048]{1,0:T(8,128)(2,1)}, bf16[64,2048]{1,0:T(8,128)(2,1)S(1)}, u32[]{:S(2)}, u32[]{:S(2)}) collective-permute-start(bf16[64,2048]{1,0:T(8,128)(2,1)} %get-tuple-element.74), channel_id=1, source_target_pairs={{0,3},{1,2},{2,1},{3,0},{4,7},{5,6},{6,5},{7,4},{8,11},{9,10},{10,... | collective-permute-start | bytes 786440 | tf_op jit(solution)/shard_map/ppermute | solution.py:15
  67.8 5.2 %collective-permute-done.15 = bf16[64,2048]{1,0:T(8,128)(2,1)S(1)} collective-permute-done((bf16[64,2048]{1,0:T(8,128)(2,1)}, bf16[64,2048]{1,0:T(8,128)(2,1)S(1)}, u32[]{:S(2)}, u32[]{:S(2)}) %collective-permute-start.15) | collective-permute-done | bytes 262176 | tf_op jit(solution)/shard_map/ppermute | solution.py:15
  72.9 0.7 copy-done.4
  73.6 0.9 collective-permute-done.14
  74.6 0.7 broadcast_in_dim.12
  75.4 6.4 %all-to-all-start.2 = ((bf16[16,16,512]{2,1,0:T(8,128)(2,1)}), bf16[16,16,512]{2,1,0:T(8,128)(2,1)S(1)}, u32[]{:S(2)}, u32[]{:S(2)}) async-start(bf16[16,16,512]{2,1,0:T(8,128)(2,1)} %bitcast.29), calls=%async_computation.2 | async-start | bytes 524288 | tf_op jit(solution)/shard_map/all_to_all | solution.py:33
  82.3 3.4 %collective-permute-start.17 = (bf16[64,2048]{1,0:T(8,128)(2,1)}, bf16[64,2048]{1,0:T(8,128)(2,1)}, u32[]{:S(2)}, u32[]{:S(2)}) collective-permute-start(bf16[64,2048]{1,0:T(8,128)(2,1)} %get-tuple-element.74), channel_id=1, source_target_pairs={{0,2},{1,3},{2,0},{3,1},{4,6},{5,7},{6,4},{7,5},{8,10},{9,11},{10,... | collective-permute-start | bytes 786440 | tf_op jit(solution)/shard_map/ppermute | solution.py:15
  85.9 6.1 %collective-permute-done.17 = bf16[64,2048]{1,0:T(8,128)(2,1)} collective-permute-done((bf16[64,2048]{1,0:T(8,128)(2,1)}, bf16[64,2048]{1,0:T(8,128)(2,1)}, u32[]{:S(2)}, u32[]{:S(2)}) %collective-permute-start.17) | collective-permute-done | bytes 262176 | tf_op jit(solution)/shard_map/ppermute | solution.py:15
  91.9 2.1 %collective-permute-done.16 = bf16[128,1856]{1,0:T(8,128)(2,1)} collective-permute-done((bf16[128,1856]{1,0:T(8,128)(2,1)S(1)}, bf16[128,1856]{1,0:T(8,128)(2,1)}, u32[]{:S(2)}, u32[]{:S(2)}) %collective-permute-start.16) | collective-permute-done | bytes 475168 | tf_op jit(solution)/shard_map/ppermute | solution.py:15
  94.3 1.3 collective-permute-done.18
  96.3 1.3 copy-done.15
  97.6 1.3 convolution_convert_fusion.1
  99.4 0.7 copy-done.1
  100.1 1.0 constant_dynamic-update-slice_fusion.6
  101.1 1.0 constant_dynamic-update-slice_fusion.5
  102.1 1.5 %collective-permute-start.23 = (bf16[64,1856]{1,0:T(8,128)(2,1)S(1)}, bf16[64,1856]{1,0:T(8,128)(2,1)S(1)}, u32[]{:S(2)}, u32[]{:S(2)}) collective-permute-start(bf16[64,1856]{1,0:T(8,128)(2,1)S(1)} %get-tuple-element.112), channel_id=1, source_target_pairs={{0,64},{32,96},{64,0},{96,32},{1,65},{33,97},{65,1},{97,33},{2,66}... | collective-permute-start | bytes 712712 | tf_op jit(solution)/shard_map/ppermute | solution.py:15
  103.5 1.7 %collective-permute-start.22 = (bf16[64,1856]{1,0:T(8,128)(2,1)S(1)}, bf16[64,1856]{1,0:T(8,128)(2,1)S(1)}, u32[]{:S(2)}, u32[]{:S(2)}) collective-permute-start(bf16[64,1856]{1,0:T(8,128)(2,1)S(1)} %get-tuple-element.113), channel_id=1, source_target_pairs={{0,32},{32,0},{64,96},{96,64},{1,33},{33,1},{65,97},{97,65},{2,34}... | collective-permute-start | bytes 712712 | tf_op jit(solution)/shard_map/ppermute | solution.py:15
  105.2 2.9 %collective-permute-start.21 = (bf16[64,1856]{1,0:T(8,128)(2,1)S(1)}, bf16[64,1856]{1,0:T(8,128)(2,1)S(1)}, u32[]{:S(2)}, u32[]{:S(2)}) collective-permute-start(bf16[64,1856]{1,0:T(8,128)(2,1)S(1)} %get-tuple-element.114), channel_id=1, source_target_pairs={{0,3},{1,2},{2,1},{3,0},{4,7},{5,6},{6,5},{7,4},{8,11},{9,10},{10,... | collective-permute-start | bytes 712712 | tf_op jit(solution)/shard_map/ppermute | solution.py:15
  108.1 0.9 collective-permute-start.20
  109.0 3.3 %collective-permute-done.24 = bf16[64,1856]{1,0:T(8,128)(2,1)S(1)} collective-permute-done((bf16[64,1856]{1,0:T(8,128)(2,1)S(1)}, bf16[64,1856]{1,0:T(8,128)(2,1)S(1)}, u32[]{:S(2)}, u32[]{:S(2)}) %collective-permute-start.24) | collective-permute-done | bytes 237600 | tf_op jit(solution)/shard_map/ppermute | solution.py:15
  112.3 1.6 %collective-permute-start.19 = (bf16[64,1856]{1,0:T(8,128)(2,1)S(1)}, bf16[64,1856]{1,0:T(8,128)(2,1)S(1)}, u32[]{:S(2)}, u32[]{:S(2)}) collective-permute-start(bf16[64,1856]{1,0:T(8,128)(2,1)S(1)} %get-tuple-element.116), channel_id=1, source_target_pairs={{0,1},{1,0},{2,3},{3,2},{4,5},{5,4},{6,7},{7,6},{8,9},{9,8},{10,11... | collective-permute-start | bytes 712712 | tf_op jit(solution)/shard_map/ppermute | solution.py:15
  114.2 2.1 %collective-permute-done.22 = bf16[64,1856]{1,0:T(8,128)(2,1)S(1)} collective-permute-done((bf16[64,1856]{1,0:T(8,128)(2,1)S(1)}, bf16[64,1856]{1,0:T(8,128)(2,1)S(1)}, u32[]{:S(2)}, u32[]{:S(2)}) %collective-permute-start.22) | collective-permute-done | bytes 237600 | tf_op jit(solution)/shard_map/ppermute | solution.py:15
  116.2 2.6 %collective-permute-done.21 = bf16[64,1856]{1,0:T(8,128)(2,1)S(1)} collective-permute-done((bf16[64,1856]{1,0:T(8,128)(2,1)S(1)}, bf16[64,1856]{1,0:T(8,128)(2,1)S(1)}, u32[]{:S(2)}, u32[]{:S(2)}) %collective-permute-start.21) | collective-permute-done | bytes 237600 | tf_op jit(solution)/shard_map/ppermute | solution.py:15
  118.9 0.6 collective-permute-done.19
  119.8 2.9 %collective-permute-start.30 = (bf16[16,1856]{1,0:T(8,128)(2,1)S(1)}, bf16[16,1856]{1,0:T(8,128)(2,1)S(1)}, u32[]{:S(2)}, u32[]{:S(2)}) collective-permute-start(bf16[16,1856]{1,0:T(8,128)(2,1)S(1)} %get-tuple-element.149), channel_id=1, source_target_pairs={{0,3},{1,2},{2,1},{3,0},{4,7},{5,6},{6,5},{7,4},{8,11},{9,10},{10,... | collective-permute-start | bytes 178184 | tf_op jit(solution)/shard_map/ppermute | solution.py:15
  122.7 0.9 collective-permute-start.29
  124.0 1.4 collective-permute-start.27
  125.3 2.3 %collective-permute-start.26 = (bf16[16,1856]{1,0:T(8,128)(2,1)S(1)}, bf16[16,1856]{1,0:T(8,128)(2,1)S(1)}, u32[]{:S(2)}, u32[]{:S(2)}) collective-permute-start(bf16[16,1856]{1,0:T(8,128)(2,1)S(1)} %get-tuple-element.153), channel_id=1, source_target_pairs={{0,64},{32,96},{64,0},{96,32},{1,65},{33,97},{65,1},{97,33},{2,66}... | collective-permute-start | bytes 178184 | tf_op jit(solution)/shard_map/ppermute | solution.py:15
  127.7 0.8 collective-permute-done.29
  128.4 1.5 %collective-permute-start.25 = (bf16[16,1856]{1,0:T(8,128)(2,1)S(1)}, bf16[16,1856]{1,0:T(8,128)(2,1)S(1)}, u32[]{:S(2)}, u32[]{:S(2)}) collective-permute-start(bf16[16,1856]{1,0:T(8,128)(2,1)S(1)} %get-tuple-element.154), channel_id=1, source_target_pairs={{0,32},{32,0},{64,96},{96,64},{1,33},{33,1},{65,97},{97,65},{2,34}... | collective-permute-start | bytes 178184 | tf_op jit(solution)/shard_map/ppermute | solution.py:15
  130.0 3.5 %convolution_convert_fusion = bf16[512,1856]{0,1:T(8,128)(2,1)} fusion(bf16[512,512]{1,0:T(8,128)(2,1)S(1)} %bitcast.150, bf16[128,1856]{1,0:T(8,128)(2,1)S(1)} %copy-done.17, bf16[128,1856]{1,0:T(8,128)(2,1)} %collective-permute-done.16, bf16[128,1856]{1,0:T(8,128)(2,1)S(1)} %copy-done.19, bf16[128,1856]{1,0:T(8,128)(2,1)S(1)} %bitcast.155), kind=kOutput, calls=%fused_computation.1 | convolution fusion | flops 981630976 | bytes 4325376 | tf_op jit(solution)/shard_map/dot_general | solution.py:27
  133.6 6.3 %collective-permute-start.32 = (bf16[16,1856]{1,0:T(8,128)(2,1)S(1)}, bf16[16,1856]{1,0:T(8,128)(2,1)S(1)}, u32[]{:S(2)}, u32[]{:S(2)}) collective-permute-start(bf16[16,1856]{1,0:T(8,128)(2,1)S(1)} %add_convert_fusion.3), channel_id=1, source_target_pairs={{0,128},{128,0},{1,129},{129,1},{2,130},{130,2},{3,131},{131,3},{4... | collective-permute-start | bytes 178184 | tf_op jit(solution)/shard_map/ppermute | solution.py:15
  139.9 0.7 fusion.36
  140.6 1.9 %add_convert_fusion = bf16[464,2048]{1,0:T(8,128)(2,1)} fusion(f32[464,2048]{1,0:T(8,128)S(1)} %fusion.36, bf16[256,464]{1,0:T(8,128)(2,1)S(1)} %bitcast.149, bf16[256,2048]{1,0:T(8,128)(2,1)S(1)} %constant_dynamic-update-slice_fusion.4), kind=kOutput, calls=%fused_computation | convolution fusion | flops 488439808 | bytes 6987776 | tf_op jit(solution)/shard_map/dot_general | solution.py:27
  142.5 0.7 add_convert_fusion.2
  (103 shorter events, 4.7 us)
Async XLA Ops:
  0.6 33.7 %copy-start = (bf16[464,2048]{1,0:T(8,128)(2,1)S(1)}, bf16[464,2048]{1,0:T(8,128)(2,1)}, u32[]{:S(2)}) copy-start(bf16[464,2048]{1,0:T(8,128)(2,1)} %param.9) | copy-start | bytes 5701636
  0.6 22.8 %copy-start.13 = (bf16[16,1856]{1,0:T(8,128)(2,1)S(1)}, bf16[16,1856]{1,0:T(8,128)(2,1)}, u32[]{:S(2)}) copy-start(bf16[16,1856]{1,0:T(8,128)(2,1)} %param.5) | copy-start | bytes 178180
  0.7 19.7 %copy-start.12 = (bf16[16,2048]{1,0:T(8,128)(2,1)S(1)}, bf16[16,2048]{1,0:T(8,128)(2,1)}, u32[]{:S(2)}) copy-start(bf16[16,2048]{1,0:T(8,128)(2,1)} %param.6) | copy-start | bytes 196612
  0.7 10.2 %collective-permute-start = (bf16[16,1856]{1,0:T(8,128)(2,1)}, bf16[16,1856]{1,0:T(8,128)(2,1)S(1)}, u32[]{:S(2)}, u32[]{:S(2)}) collective-permute-start(bf16[16,1856]{1,0:T(8,128)(2,1)} %param.7), channel_id=1, source_target_pairs={{0,128},{128,0},{1,129},{129,1},{2,130},{130,2},{3,131},{131,3},{4... | collective-permute-start | bytes 178184 | tf_op jit(solution)/shard_map/ppermute | solution.py:15
  7.9 15.5 %collective-permute-start.1 = (bf16[16,1856]{1,0:T(8,128)(2,1)}, bf16[16,1856]{1,0:T(8,128)(2,1)S(1)}, u32[]{:S(2)}, u32[]{:S(2)}) collective-permute-start(bf16[16,1856]{1,0:T(8,128)(2,1)} %param.5), channel_id=1, source_target_pairs={{0,128},{128,0},{1,129},{129,1},{2,130},{130,2},{3,131},{131,3},{4... | collective-permute-start | bytes 178184 | tf_op jit(solution)/shard_map/ppermute | solution.py:15
  13.0 20.6 %all-to-all-start = ((bf16[16,32,464]{2,1,0:T(8,128)(2,1)}), bf16[16,32,464]{2,1,0:T(8,128)(2,1)S(1)}, u32[]{:S(2)}, u32[]{:S(2)}) async-start(bf16[16,32,464]{2,1,0:T(8,128)(2,1)} %bitcast.1), calls=%async_computation | async-start | bytes 1048576 | tf_op jit(solution)/shard_map/all_to_all | solution.py:33
  20.4 8.8 %collective-permute-start.7 = (bf16[16,2048]{1,0:T(8,128)(2,1)S(1)}, bf16[16,2048]{1,0:T(8,128)(2,1)S(1)}, u32[]{:S(2)}, u32[]{:S(2)}) collective-permute-start(bf16[16,2048]{1,0:T(8,128)(2,1)S(1)} %get-tuple-element.56), channel_id=1, source_target_pairs={{0,24},{8,16},{16,8},{24,0},{1,25},{9,17},{17,9},{25,1},{2,26},{10... | collective-permute-start | bytes 196616 | tf_op jit(solution)/shard_map/ppermute | solution.py:15
  23.4 10.1 %collective-permute-start.4 = (bf16[2,16,1856]{2,1,0:T(8,128)(2,1)S(1)}, bf16[2,16,1856]{2,1,0:T(8,128)(2,1)S(1)}, u32[]{:S(2)}, u32[]{:S(2)}) collective-permute-start(bf16[2,16,1856]{2,1,0:T(8,128)(2,1)S(1)} %get-tuple-element.156), channel_id=1, source_target_pairs={{0,3},{1,2},{2,1},{3,0},{4,7},{5,6},{6,5},{7,4},{8,11},{9,10},{10,... | collective-permute-start | bytes 356360 | tf_op jit(solution)/shard_map/ppermute | solution.py:15
  26.2 7.3 %collective-permute-start.3 = (bf16[2,16,1856]{2,1,0:T(8,128)(2,1)S(1)}, bf16[2,16,1856]{2,1,0:T(8,128)(2,1)S(1)}, u32[]{:S(2)}, u32[]{:S(2)}) collective-permute-start(bf16[2,16,1856]{2,1,0:T(8,128)(2,1)S(1)} %get-tuple-element.156), channel_id=1, source_target_pairs={{0,2},{1,3},{2,0},{3,1},{4,6},{5,7},{6,4},{7,5},{8,10},{9,11},{10,... | collective-permute-start | bytes 356360 | tf_op jit(solution)/shard_map/ppermute | solution.py:15
  27.1 6.5 %collective-permute-start.2 = (bf16[2,16,1856]{2,1,0:T(8,128)(2,1)S(1)}, bf16[2,16,1856]{2,1,0:T(8,128)(2,1)}, u32[]{:S(2)}, u32[]{:S(2)}) collective-permute-start(bf16[2,16,1856]{2,1,0:T(8,128)(2,1)S(1)} %get-tuple-element.156), channel_id=1, source_target_pairs={{0,1},{1,0},{2,3},{3,2},{4,5},{5,4},{6,7},{7,6},{8,9},{9,8},{10,11... | collective-permute-start | bytes 356360 | tf_op jit(solution)/shard_map/ppermute | solution.py:15
  27.6 5.2 %collective-permute-start.6 = (bf16[16,2048]{1,0:T(8,128)(2,1)S(1)}, bf16[16,2048]{1,0:T(8,128)(2,1)S(1)}, u32[]{:S(2)}, u32[]{:S(2)}) collective-permute-start(bf16[16,2048]{1,0:T(8,128)(2,1)S(1)} %get-tuple-element.56), channel_id=1, source_target_pairs={{0,16},{8,24},{16,0},{24,8},{1,17},{9,25},{17,1},{25,9},{2,18},{10... | collective-permute-start | bytes 196616 | tf_op jit(solution)/shard_map/ppermute | solution.py:15
  29.2 4.3 %copy-start.6 = (bf16[16,2048]{1,0:T(8,128)(2,1)}, bf16[16,2048]{1,0:T(8,128)(2,1)S(1)}, u32[]{:S(2)}) copy-start(bf16[16,2048]{1,0:T(8,128)(2,1)S(1)} %collective-permute-done.7) | copy-start | bytes 196612
  29.2 4.3 %collective-permute-start.5 = (bf16[16,2048]{1,0:T(8,128)(2,1)S(1)}, bf16[16,2048]{1,0:T(8,128)(2,1)S(1)}, u32[]{:S(2)}, u32[]{:S(2)}) collective-permute-start(bf16[16,2048]{1,0:T(8,128)(2,1)S(1)} %get-tuple-element.56), channel_id=1, source_target_pairs={{0,8},{8,0},{16,24},{24,16},{1,9},{9,1},{17,25},{25,17},{2,10},{10... | collective-permute-start | bytes 196616 | tf_op jit(solution)/shard_map/ppermute | solution.py:15
  32.8 0.8 copy-start.8
  33.5 0.6 copy-start.10
  36.0 3.0 %collective-permute-start.8 = (bf16[256,2048]{1,0:T(8,128)(2,1)}, bf16[256,2048]{1,0:T(8,128)(2,1)}, u32[]{:S(2)}, u32[]{:S(2)}) collective-permute-start(bf16[256,2048]{1,0:T(8,128)(2,1)} %convolution_convert_fusion.2), channel_id=1, source_target_pairs={{0,4},{4,0},{1,5},{5,1},{2,6},{6,2},{3,7},{7,3},{8,12},{12,8},{9,1... | collective-permute-start | bytes 3145736 | tf_op jit(solution)/shard_map/ppermute | solution.py:15
  37.6 4.9 %copy-start.2 = (bf16[4,2,16,1856]{3,2,1,0:T(8,128)(2,1)}, bf16[4,2,16,1856]{3,2,1,0:T(8,128)(2,1)S(1)}, u32[]{:S(2)}) copy-start(bf16[4,2,16,1856]{3,2,1,0:T(8,128)(2,1)S(1)} %pad_maximum_fusion.7) | copy-start | bytes 1425412
  37.6 10.9 %copy-start.11 = (bf16[16,2048]{1,0:T(8,128)(2,1)S(1)}, bf16[16,2048]{1,0:T(8,128)(2,1)}, u32[]{:S(2)}) copy-start(bf16[16,2048]{1,0:T(8,128)(2,1)} %copy-done.10) | copy-start | bytes 196612
  37.6 11.5 %copy-start.9 = (bf16[16,2048]{1,0:T(8,128)(2,1)S(1)}, bf16[16,2048]{1,0:T(8,128)(2,1)}, u32[]{:S(2)}) copy-start(bf16[16,2048]{1,0:T(8,128)(2,1)} %copy-done.8) | copy-start | bytes 196612
  40.9 23.2 %copy-start.7 = (bf16[16,2048]{1,0:T(8,128)(2,1)S(1)}, bf16[16,2048]{1,0:T(8,128)(2,1)}, u32[]{:S(2)}) copy-start(bf16[16,2048]{1,0:T(8,128)(2,1)} %copy-done.6) | copy-start | bytes 196612
  41.0 18.7 %collective-permute-start.13 = (bf16[128,1856]{1,0:T(8,128)(2,1)S(1)}, bf16[128,1856]{1,0:T(8,128)(2,1)S(1)}, u32[]{:S(2)}, u32[]{:S(2)}) collective-permute-start(bf16[128,1856]{1,0:T(8,128)(2,1)S(1)} %bitcast.152), channel_id=1, source_target_pairs={{0,96},{32,64},{64,32},{96,0},{1,97},{33,65},{65,33},{97,1},{2,98}... | collective-permute-start | bytes 1425416 | tf_op jit(solution)/shard_map/ppermute | solution.py:15
  42.5 17.2 %collective-permute-start.12 = (bf16[128,1856]{1,0:T(8,128)(2,1)S(1)}, bf16[128,1856]{1,0:T(8,128)(2,1)S(1)}, u32[]{:S(2)}, u32[]{:S(2)}) collective-permute-start(bf16[128,1856]{1,0:T(8,128)(2,1)S(1)} %bitcast.153), channel_id=1, source_target_pairs={{0,32},{32,0},{64,96},{96,64},{1,33},{33,1},{65,97},{97,65},{2,34}... | collective-permute-start | bytes 1425416 | tf_op jit(solution)/shard_map/ppermute | solution.py:15
  44.4 14.7 %collective-permute-start.11 = (bf16[64,2048]{1,0:T(8,128)(2,1)S(1)}, bf16[64,2048]{1,0:T(8,128)(2,1)S(1)}, u32[]{:S(2)}, u32[]{:S(2)}) collective-permute-start(bf16[64,2048]{1,0:T(8,128)(2,1)S(1)} %get-tuple-element.117), channel_id=1, source_target_pairs={{0,3},{1,2},{2,1},{3,0},{4,7},{5,6},{6,5},{7,4},{8,11},{9,10},{10,... | collective-permute-start | bytes 786440 | tf_op jit(solution)/shard_map/ppermute | solution.py:15
  47.1 11.9 %collective-permute-start.10 = (bf16[64,2048]{1,0:T(8,128)(2,1)S(1)}, bf16[64,2048]{1,0:T(8,128)(2,1)S(1)}, u32[]{:S(2)}, u32[]{:S(2)}) collective-permute-start(bf16[64,2048]{1,0:T(8,128)(2,1)S(1)} %get-tuple-element.118), channel_id=1, source_target_pairs={{0,2},{1,3},{2,0},{3,1},{4,6},{5,7},{6,4},{7,5},{8,10},{9,11},{10,... | collective-permute-start | bytes 786440 | tf_op jit(solution)/shard_map/ppermute | solution.py:15
  48.0 11.7 %collective-permute-start.9 = (bf16[64,2048]{1,0:T(8,128)(2,1)S(1)}, bf16[64,2048]{1,0:T(8,128)(2,1)S(1)}, u32[]{:S(2)}, u32[]{:S(2)}) collective-permute-start(bf16[64,2048]{1,0:T(8,128)(2,1)S(1)} %get-tuple-element.119), channel_id=1, source_target_pairs={{0,1},{1,0},{2,3},{3,2},{4,5},{5,4},{6,7},{7,6},{8,9},{9,8},{10,11... | collective-permute-start | bytes 786440 | tf_op jit(solution)/shard_map/ppermute | solution.py:15
  49.8 10.9 %copy-start.14 = (bf16[64,2048]{1,0:T(8,128)(2,1)}, bf16[64,2048]{1,0:T(8,128)(2,1)S(1)}, u32[]{:S(2)}) copy-start(bf16[64,2048]{1,0:T(8,128)(2,1)S(1)} %get-tuple-element.162) | copy-start | bytes 786436
  49.8 32.0 %copy-start.3 = (bf16[4,2,16,1856]{3,2,1,0:T(8,128)(2,1)S(1)}, bf16[4,2,16,1856]{3,2,1,0:T(8,128)(2,1)}, u32[]{:S(2)}) copy-start(bf16[4,2,16,1856]{3,2,1,0:T(8,128)(2,1)} %copy-done.2) | copy-start | bytes 1425412
  59.7 1.0 copy-start.16
  59.7 1.1 copy-start.18
  60.8 13.8 %all-to-all-start.1 = ((bf16[4,16,2048]{2,1,0:T(8,128)(2,1)}), bf16[4,16,2048]{2,1,0:T(8,128)(2,1)S(1)}, u32[]{:S(2)}, u32[]{:S(2)}) async-start(bf16[4,16,2048]{2,1,0:T(8,128)(2,1)} %bitcast.26), calls=%async_computation.1 | async-start | bytes 524288 | tf_op jit(solution)/shard_map/all_to_all | solution.py:33
  64.8 8.1 %collective-permute-start.15 = (bf16[64,2048]{1,0:T(8,128)(2,1)}, bf16[64,2048]{1,0:T(8,128)(2,1)S(1)}, u32[]{:S(2)}, u32[]{:S(2)}) collective-permute-start(bf16[64,2048]{1,0:T(8,128)(2,1)} %get-tuple-element.74), channel_id=1, source_target_pairs={{0,3},{1,2},{2,1},{3,0},{4,7},{5,6},{6,5},{7,4},{8,11},{9,10},{10,... | collective-permute-start | bytes 786440 | tf_op jit(solution)/shard_map/ppermute | solution.py:15
  67.5 7.0 %collective-permute-start.14 = (bf16[64,2048]{1,0:T(8,128)(2,1)}, bf16[64,2048]{1,0:T(8,128)(2,1)}, u32[]{:S(2)}, u32[]{:S(2)}) collective-permute-start(bf16[64,2048]{1,0:T(8,128)(2,1)} %get-tuple-element.74), channel_id=1, source_target_pairs={{0,1},{1,0},{2,3},{3,2},{4,5},{5,4},{6,7},{7,6},{8,9},{9,8},{10,11... | collective-permute-start | bytes 786440 | tf_op jit(solution)/shard_map/ppermute | solution.py:15
  72.9 0.7 copy-start.4
  75.4 18.7 %all-to-all-start.2 = ((bf16[16,16,512]{2,1,0:T(8,128)(2,1)}), bf16[16,16,512]{2,1,0:T(8,128)(2,1)S(1)}, u32[]{:S(2)}, u32[]{:S(2)}) async-start(bf16[16,16,512]{2,1,0:T(8,128)(2,1)} %bitcast.29), calls=%async_computation.2 | async-start | bytes 524288 | tf_op jit(solution)/shard_map/all_to_all | solution.py:33
  81.8 12.3 %collective-permute-start.16 = (bf16[128,1856]{1,0:T(8,128)(2,1)S(1)}, bf16[128,1856]{1,0:T(8,128)(2,1)}, u32[]{:S(2)}, u32[]{:S(2)}) collective-permute-start(bf16[128,1856]{1,0:T(8,128)(2,1)S(1)} %bitcast.154), channel_id=1, source_target_pairs={{0,64},{32,96},{64,0},{96,32},{1,65},{33,97},{65,1},{97,33},{2,66}... | collective-permute-start | bytes 1425416 | tf_op jit(solution)/shard_map/ppermute | solution.py:15
  82.3 9.6 %collective-permute-start.17 = (bf16[64,2048]{1,0:T(8,128)(2,1)}, bf16[64,2048]{1,0:T(8,128)(2,1)}, u32[]{:S(2)}, u32[]{:S(2)}) collective-permute-start(bf16[64,2048]{1,0:T(8,128)(2,1)} %get-tuple-element.74), channel_id=1, source_target_pairs={{0,2},{1,3},{2,0},{3,1},{4,6},{5,7},{6,4},{7,5},{8,10},{9,11},{10,... | collective-permute-start | bytes 786440 | tf_op jit(solution)/shard_map/ppermute | solution.py:15
  94.1 1.5 %collective-permute-start.18 = (bf16[16,16,512]{2,1,0:T(8,128)(2,1)S(1)}, bf16[16,16,512]{2,1,0:T(8,128)(2,1)S(1)}, u32[]{:S(2)}, u32[]{:S(2)}) collective-permute-start(bf16[16,16,512]{2,1,0:T(8,128)(2,1)S(1)} %all-to-all-done.2), channel_id=1, source_target_pairs={{0,4},{4,0},{1,5},{5,1},{2,6},{6,2},{3,7},{7,3},{8,12},{12,8},{9,1... | collective-permute-start | bytes 786440 | tf_op jit(solution)/shard_map/ppermute | solution.py:15
  96.1 1.5 %copy-start.15 = (bf16[512,1856]{0,1:T(8,128)(2,1)S(1)}, bf16[512,1856]{0,1:T(8,128)(2,1)}, u32[]{:S(2)}) copy-start(bf16[512,1856]{0,1:T(8,128)(2,1)} %param.8) | copy-start | bytes 5701636
  98.9 1.2 copy-start.1
  98.9 15.0 %copy-start.5 = (bf16[64,2048]{1,0:T(8,128)(2,1)S(1)}, bf16[64,2048]{1,0:T(8,128)(2,1)}, u32[]{:S(2)}) copy-start(bf16[64,2048]{1,0:T(8,128)(2,1)} %copy-done.4) | copy-start | bytes 786436
  99.0 13.2 %collective-permute-start.24 = (bf16[64,1856]{1,0:T(8,128)(2,1)S(1)}, bf16[64,1856]{1,0:T(8,128)(2,1)S(1)}, u32[]{:S(2)}, u32[]{:S(2)}) collective-permute-start(bf16[64,1856]{1,0:T(8,128)(2,1)S(1)} %get-tuple-element.111), channel_id=1, source_target_pairs={{0,96},{32,64},{64,32},{96,0},{1,97},{33,65},{65,33},{97,1},{2,98}... | collective-permute-start | bytes 712712 | tf_op jit(solution)/shard_map/ppermute | solution.py:15
  102.1 12.0 %collective-permute-start.23 = (bf16[64,1856]{1,0:T(8,128)(2,1)S(1)}, bf16[64,1856]{1,0:T(8,128)(2,1)S(1)}, u32[]{:S(2)}, u32[]{:S(2)}) collective-permute-start(bf16[64,1856]{1,0:T(8,128)(2,1)S(1)} %get-tuple-element.112), channel_id=1, source_target_pairs={{0,64},{32,96},{64,0},{96,32},{1,65},{33,97},{65,1},{97,33},{2,66}... | collective-permute-start | bytes 712712 | tf_op jit(solution)/shard_map/ppermute | solution.py:15
  103.5 12.7 %collective-permute-start.22 = (bf16[64,1856]{1,0:T(8,128)(2,1)S(1)}, bf16[64,1856]{1,0:T(8,128)(2,1)S(1)}, u32[]{:S(2)}, u32[]{:S(2)}) collective-permute-start(bf16[64,1856]{1,0:T(8,128)(2,1)S(1)} %get-tuple-element.113), channel_id=1, source_target_pairs={{0,32},{32,0},{64,96},{96,64},{1,33},{33,1},{65,97},{97,65},{2,34}... | collective-permute-start | bytes 712712 | tf_op jit(solution)/shard_map/ppermute | solution.py:15
  105.2 13.6 %collective-permute-start.21 = (bf16[64,1856]{1,0:T(8,128)(2,1)S(1)}, bf16[64,1856]{1,0:T(8,128)(2,1)S(1)}, u32[]{:S(2)}, u32[]{:S(2)}) collective-permute-start(bf16[64,1856]{1,0:T(8,128)(2,1)S(1)} %get-tuple-element.114), channel_id=1, source_target_pairs={{0,3},{1,2},{2,1},{3,0},{4,7},{5,6},{6,5},{7,4},{8,11},{9,10},{10,... | collective-permute-start | bytes 712712 | tf_op jit(solution)/shard_map/ppermute | solution.py:15
  108.1 10.8 %collective-permute-start.20 = (bf16[64,1856]{1,0:T(8,128)(2,1)S(1)}, bf16[64,1856]{1,0:T(8,128)(2,1)S(1)}, u32[]{:S(2)}, u32[]{:S(2)}) collective-permute-start(bf16[64,1856]{1,0:T(8,128)(2,1)S(1)} %get-tuple-element.115), channel_id=1, source_target_pairs={{0,2},{1,3},{2,0},{3,1},{4,6},{5,7},{6,4},{7,5},{8,10},{9,11},{10,... | collective-permute-start | bytes 712712 | tf_op jit(solution)/shard_map/ppermute | solution.py:15
  112.3 7.2 %collective-permute-start.19 = (bf16[64,1856]{1,0:T(8,128)(2,1)S(1)}, bf16[64,1856]{1,0:T(8,128)(2,1)S(1)}, u32[]{:S(2)}, u32[]{:S(2)}) collective-permute-start(bf16[64,1856]{1,0:T(8,128)(2,1)S(1)} %get-tuple-element.116), channel_id=1, source_target_pairs={{0,1},{1,0},{2,3},{3,2},{4,5},{5,4},{6,7},{7,6},{8,9},{9,8},{10,11... | collective-permute-start | bytes 712712 | tf_op jit(solution)/shard_map/ppermute | solution.py:15
  114.0 16.0 %copy-start.17 = (bf16[128,1856]{1,0:T(8,128)(2,1)S(1)}, bf16[128,1856]{1,0:T(8,128)(2,1)}, u32[]{:S(2)}) copy-start(bf16[128,1856]{1,0:T(8,128)(2,1)} %copy-done.16) | copy-start | bytes 1425412
  114.0 16.0 %copy-start.19 = (bf16[128,1856]{1,0:T(8,128)(2,1)S(1)}, bf16[128,1856]{1,0:T(8,128)(2,1)}, u32[]{:S(2)}) copy-start(bf16[128,1856]{1,0:T(8,128)(2,1)} %copy-done.18) | copy-start | bytes 1425412
  114.1 19.4 %collective-permute-start.31 = (bf16[256,2048]{1,0:T(8,128)(2,1)S(1)}, bf16[256,2048]{1,0:T(8,128)(2,1)S(1)}, u32[]{:S(2)}, u32[]{:S(2)}) collective-permute-start(bf16[256,2048]{1,0:T(8,128)(2,1)S(1)} %constant_dynamic-update-slice_fusion.4), channel_id=1, source_target_pairs={{0,4},{4,0},{1,5},{5,1},{2,6},{6,2},{3,7},{7,3},{8,12},{12,8},{9,1... | collective-permute-start | bytes 3145736 | tf_op jit(solution)/shard_map/ppermute | solution.py:15
  119.8 5.6 %collective-permute-start.30 = (bf16[16,1856]{1,0:T(8,128)(2,1)S(1)}, bf16[16,1856]{1,0:T(8,128)(2,1)S(1)}, u32[]{:S(2)}, u32[]{:S(2)}) collective-permute-start(bf16[16,1856]{1,0:T(8,128)(2,1)S(1)} %get-tuple-element.149), channel_id=1, source_target_pairs={{0,3},{1,2},{2,1},{3,0},{4,7},{5,6},{6,5},{7,4},{8,11},{9,10},{10,... | collective-permute-start | bytes 178184 | tf_op jit(solution)/shard_map/ppermute | solution.py:15
  122.7 5.7 %collective-permute-start.29 = (bf16[16,1856]{1,0:T(8,128)(2,1)S(1)}, bf16[16,1856]{1,0:T(8,128)(2,1)S(1)}, u32[]{:S(2)}, u32[]{:S(2)}) collective-permute-start(bf16[16,1856]{1,0:T(8,128)(2,1)S(1)} %get-tuple-element.150), channel_id=1, source_target_pairs={{0,2},{1,3},{2,0},{3,1},{4,6},{5,7},{6,4},{7,5},{8,10},{9,11},{10,... | collective-permute-start | bytes 178184 | tf_op jit(solution)/shard_map/ppermute | solution.py:15
  123.6 9.9 %collective-permute-start.28 = (bf16[16,1856]{1,0:T(8,128)(2,1)S(1)}, bf16[16,1856]{1,0:T(8,128)(2,1)S(1)}, u32[]{:S(2)}, u32[]{:S(2)}) collective-permute-start(bf16[16,1856]{1,0:T(8,128)(2,1)S(1)} %get-tuple-element.151), channel_id=1, source_target_pairs={{0,1},{1,0},{2,3},{3,2},{4,5},{5,4},{6,7},{7,6},{8,9},{9,8},{10,11... | collective-permute-start | bytes 178184 | tf_op jit(solution)/shard_map/ppermute | solution.py:15
  124.0 9.5 %collective-permute-start.27 = (bf16[16,1856]{1,0:T(8,128)(2,1)S(1)}, bf16[16,1856]{1,0:T(8,128)(2,1)S(1)}, u32[]{:S(2)}, u32[]{:S(2)}) collective-permute-start(bf16[16,1856]{1,0:T(8,128)(2,1)S(1)} %get-tuple-element.152), channel_id=1, source_target_pairs={{0,96},{32,64},{64,32},{96,0},{1,97},{33,65},{65,33},{97,1},{2,98}... | collective-permute-start | bytes 178184 | tf_op jit(solution)/shard_map/ppermute | solution.py:15
  125.3 8.2 %collective-permute-start.26 = (bf16[16,1856]{1,0:T(8,128)(2,1)S(1)}, bf16[16,1856]{1,0:T(8,128)(2,1)S(1)}, u32[]{:S(2)}, u32[]{:S(2)}) collective-permute-start(bf16[16,1856]{1,0:T(8,128)(2,1)S(1)} %get-tuple-element.153), channel_id=1, source_target_pairs={{0,64},{32,96},{64,0},{96,32},{1,65},{33,97},{65,1},{97,33},{2,66}... | collective-permute-start | bytes 178184 | tf_op jit(solution)/shard_map/ppermute | solution.py:15
  128.4 5.1 %collective-permute-start.25 = (bf16[16,1856]{1,0:T(8,128)(2,1)S(1)}, bf16[16,1856]{1,0:T(8,128)(2,1)S(1)}, u32[]{:S(2)}, u32[]{:S(2)}) collective-permute-start(bf16[16,1856]{1,0:T(8,128)(2,1)S(1)} %get-tuple-element.154), channel_id=1, source_target_pairs={{0,32},{32,0},{64,96},{96,64},{1,33},{33,1},{65,97},{97,65},{2,34}... | collective-permute-start | bytes 178184 | tf_op jit(solution)/shard_map/ppermute | solution.py:15
  133.6 9.0 %collective-permute-start.32 = (bf16[16,1856]{1,0:T(8,128)(2,1)S(1)}, bf16[16,1856]{1,0:T(8,128)(2,1)S(1)}, u32[]{:S(2)}, u32[]{:S(2)}) collective-permute-start(bf16[16,1856]{1,0:T(8,128)(2,1)S(1)} %add_convert_fusion.3), channel_id=1, source_target_pairs={{0,128},{128,0},{1,129},{129,1},{2,130},{130,2},{3,131},{131,3},{4... | collective-permute-start | bytes 178184 | tf_op jit(solution)/shard_map/ppermute | solution.py:15
where the time goes:
time: 144 us; the launch traced here: 143 us
  starting transfers between devices  72.5 us (50%)
  waiting for transfers between devices  43.3 us (30%)
  matrix products  11 us (8%)
  local copies, waits for them, and re-layouts  10.6 us (7%)
  other arithmetic  4.6 us (3%)
    ppermute x33, starting transfers between devices, flip(): return lax.ppermute(value, axes, [(i, i ^ bits) for i in range(size)])  55.3 us
    ppermute x33, waiting for transfers between devices, flip(): return lax.ppermute(value, axes, [(i, i ^ bits) for i in range(size)])  43.3 us
    all_to_all x3, starting transfers between devices, exchange(): return lax.all_to_all(blocks, axes, 0, 0, tiled=True)  17.2 us
    unnamed x46, local copies, waits for them, and re-layouts  7.91 us
    dot_general x3, matrix products, over_tokens(): lax.dot_general(left, right, (((0,), (0,)), ((), ())), preferred_element_...  6.11 us
    dot_general x3, matrix products, dot(): return jnp.dot(left, right, preferred_element_type=jnp.float32)  4.9 us
  transfers between devices with their start and end apart: 36, of which 16 were waited for; matrix products, arithmetic and copies ran while one was open for 10% of the time, Pallas kernels for 0%

commit v1 on v0

--- a/solution.py
+++ b/solution.py
@@ -47,10 +47,6 @@
     return lax.optimization_barrier(transfers)
 
 
-def after(value, other):
-    return lax.optimization_barrier((value, other))[0]
-
-
 def pick(blocks, index):
     return lax.dynamic_index_in_dim(blocks, index, 0, keepdims=False)
 
@@ -85,7 +81,6 @@
     slope, act = lax.optimization_barrier((slope, act))
 
     dy = ordered(grad_out, flip(grad_out, "zh", 1, ZH), zh)
-    act_send = after(act, dy)
     x_pair = jnp.stack([inputs, flip(inputs, "zh", 1, ZH)])
 
     dy = dy.reshape(ZH, rows, X, part).transpose(2, 0, 1, 3)
@@ -93,7 +88,7 @@
     dy, x_far, act_far = beside(
         exchange(dy, ("y",) + DEPTH),
         [over_x(x_pair, k) for k in (1, 2, 3)],
-        [flip(act_send, "zl", k, ZL) for k in (1, 2, 3)],
+        [flip(act, "zl", k, ZL) for k in (1, 2, 3)],
     )
     x_rows = jnp.stack([x_pair] + x_far).reshape(-1, feats)
     act = jnp.concatenate([act] + act_far)
@@ -103,19 +98,17 @@
     dy_x = relative(dy.transpose(1, 0, 2, 3), x).transpose(1, 0, 2, 3)
     dy_x = dy_x.reshape(CORE, X * ZL * rows, part)
     theirs = dot(pick(dy_x, 1 - core), w_out).astype(jnp.bfloat16)
-    sums = dot(pick(dy_x, core), w_out) + wide(flip(theirs, "core", 1, CORE))
+    theirs, x_rows = beside(flip(theirs, "core", 1, CORE), x_rows)
+    sums = dot(pick(dy_x, core), w_out) + wide(theirs)
     sums = sums.astype(jnp.bfloat16).reshape(X, ZL * rows, hid)
-    sums, x_rows = lax.optimization_barrier((sums, x_rows))
 
-    y_rows = after(x_rows, sums)
     others, x_one, x_three = beside(
-        [over_x(sums[k], k) for k in (1, 2, 3)], over_y(y_rows, 1), over_y(y_rows, 3)
+        [over_x(sums[k], k) for k in (1, 2, 3)], over_y(x_rows, 1), over_y(x_rows, 3)
     )
     sums = plus(sums[0], others).astype(jnp.bfloat16).reshape(ZL, rows, hid)
 
-    send = after(act, sums)
     act_grad, act_one, act_three = beside(
-        exchange(sums, ("zl",)), over_x(send, 1), over_x(send, 3)
+        exchange(sums, ("zl",)), over_x(act, 1), over_x(act, 3)
     )
 
     hid_grad = (added(act_grad) * slope).astype(jnp.bfloat16)
@@ -123,8 +116,8 @@
     dz = jnp.broadcast_to(dz, (X, ZL, rows, hid_part)).reshape(X * ZL, rows, hid_part)
     dz, x_two, act_two = beside(
         exchange(dz, DEPTH + ("zl",)),
-        over_y(after(x_rows, dz), 2),
-        over_x(after(act, dz), 2),
+        over_y(x_rows, 2),
+        over_x(act, 2),
     )
     dz = ordered(dz, flip(dz, "core", 1, CORE), core)
     dz = dz.reshape(CORE, X, ZH, Y // 2, rows, hid_part)

time: 144 us -> 143 us (level)
  other arithmetic: 4.6 us -> 6.14 us
    convert_element_type x0 -> x1, other arithmetic: none -> 1.54 us  [body(): sums = sums.astype(jnp.bfloat16).reshape(X, ZL * rows, hid)]
  transfers between devices with their start and end apart: 36 -> 36, of which waited for: 16 -> 16; matrix products, arithmetic and copies ran while one was open for 10% -> 12% of each run, Pallas kernels for 0% -> 0%
where the time goes in v1:
time: 143 us
  starting transfers between devices  72.2 us (50%)
  waiting for transfers between devices  42.7 us (30%)
  local copies, waits for them, and re-layouts  10.6 us (7%)
  matrix products  9.79 us (7%)
  other arithmetic  6.14 us (4%)
    ppermute x33, starting transfers between devices, flip(): return lax.ppermute(value, axes, [(i, i ^ bits) for i in range(size)])  55 us
    ppermute x33, waiting for transfers between devices, flip(): return lax.ppermute(value, axes, [(i, i ^ bits) for i in range(size)])  42.7 us
    all_to_all x3, starting transfers between devices, exchange(): return lax.all_to_all(blocks, axes, 0, 0, tiled=True)  17.2 us
    unnamed x46, local copies, waits for them, and re-layouts  7.89 us
    dot_general x3, matrix products, over_tokens(): lax.dot_general(left, right, (((0,), (0,)), ((), ())), preferred_element_...  6.11 us
    dot_general x3, matrix products, dot(): return jnp.dot(left, right, preferred_element_type=jnp.float32)  3.67 us
  transfers between devices with their start and end apart: 36, of which 16 were waited for; matrix products, arithmetic and copies ran while one was open for 12% of the time, Pallas kernels for 0%

profile of v1, /device:TPU:8, one launch (start us, length us, event | category | flops | bytes accessed | tf_op | source)
XLA Modules:
  0.0 142.6 jit_solution(748424716732754741)
XLA Ops:
  0.7 7.3 %collective-permute-start = (bf16[16,1856]{1,0:T(8,128)(2,1)}, bf16[16,1856]{1,0:T(8,128)(2,1)S(1)}, u32[]{:S(2)}, u32[]{:S(2)}) collective-permute-start(bf16[16,1856]{1,0:T(8,128)(2,1)} %param.7), channel_id=1, source_target_pairs={{0,128},{128,0},{1,129},{129,1},{2,130},{130,2},{3,131},{131,3},{4... | collective-permute-start | bytes 178184 | tf_op jit(solution)/shard_map/ppermute | solution.py:15
  8.0 2.8 %collective-permute-done = bf16[16,1856]{1,0:T(8,128)(2,1)S(1)} collective-permute-done((bf16[16,1856]{1,0:T(8,128)(2,1)}, bf16[16,1856]{1,0:T(8,128)(2,1)S(1)}, u32[]{:S(2)}, u32[]{:S(2)}) %collective-permute-start) | collective-permute-done | bytes 59424 | tf_op jit(solution)/shard_map/ppermute | solution.py:15
  10.8 0.8 broadcast_select_fusion.3
  12.1 0.9 broadcast_in_dim.10
  13.0 7.4 %all-to-all-start = ((bf16[16,32,464]{2,1,0:T(8,128)(2,1)}), bf16[16,32,464]{2,1,0:T(8,128)(2,1)S(1)}, u32[]{:S(2)}, u32[]{:S(2)}) async-start(bf16[16,32,464]{2,1,0:T(8,128)(2,1)} %bitcast.1), calls=%async_computation | async-start | bytes 1048576 | tf_op jit(solution)/shard_map/all_to_all | solution.py:33
  20.4 3.0 %collective-permute-start.7 = (bf16[16,2048]{1,0:T(8,128)(2,1)S(1)}, bf16[16,2048]{1,0:T(8,128)(2,1)S(1)}, u32[]{:S(2)}, u32[]{:S(2)}) collective-permute-start(bf16[16,2048]{1,0:T(8,128)(2,1)S(1)} %get-tuple-element.52), channel_id=1, source_target_pairs={{0,24},{8,16},{16,8},{24,0},{1,25},{9,17},{17,9},{25,1},{2,26},{10... | collective-permute-start | bytes 196616 | tf_op jit(solution)/shard_map/ppermute | solution.py:15
  23.4 2.8 %collective-permute-start.4 = (bf16[2,16,1856]{2,1,0:T(8,128)(2,1)S(1)}, bf16[2,16,1856]{2,1,0:T(8,128)(2,1)S(1)}, u32[]{:S(2)}, u32[]{:S(2)}) collective-permute-start(bf16[2,16,1856]{2,1,0:T(8,128)(2,1)S(1)} %get-tuple-element.148), channel_id=1, source_target_pairs={{0,3},{1,2},{2,1},{3,0},{4,7},{5,6},{6,5},{7,4},{8,11},{9,10},{10,... | collective-permute-start | bytes 356360 | tf_op jit(solution)/shard_map/ppermute | solution.py:15
  26.2 0.9 collective-permute-start.3
  27.6 1.6 %collective-permute-start.6 = (bf16[16,2048]{1,0:T(8,128)(2,1)S(1)}, bf16[16,2048]{1,0:T(8,128)(2,1)S(1)}, u32[]{:S(2)}, u32[]{:S(2)}) collective-permute-start(bf16[16,2048]{1,0:T(8,128)(2,1)S(1)} %get-tuple-element.52), channel_id=1, source_target_pairs={{0,16},{8,24},{16,0},{24,8},{1,17},{9,25},{17,1},{25,9},{2,18},{10... | collective-permute-start | bytes 196616 | tf_op jit(solution)/shard_map/ppermute | solution.py:15
  29.3 3.5 %collective-permute-done.6 = bf16[16,2048]{1,0:T(8,128)(2,1)S(1)} collective-permute-done((bf16[16,2048]{1,0:T(8,128)(2,1)S(1)}, bf16[16,2048]{1,0:T(8,128)(2,1)S(1)}, u32[]{:S(2)}, u32[]{:S(2)}) %collective-permute-start.6) | collective-permute-done | bytes 65568 | tf_op jit(solution)/shard_map/ppermute | solution.py:15
  32.8 0.7 collective-permute-done.5
  33.6 0.6 copy-done.10
  34.3 1.7 %convolution_convert_fusion.2 = bf16[256,2048]{1,0:T(8,128)(2,1)} fusion(bf16[464,2048]{1,0:T(8,128)(2,1)S(1)} %copy-done, bf16[2,256,464]{2,1,0:T(8,128)(2,1)S(1)} %bitcast.128, s32[]{:T(128)S(6)} %select_n.97), kind=kOutput, calls=%fused_computation.3 | convolution fusion | flops 487063552 | bytes 3211268 | tf_op jit(solution)/shard_map/dot_general | solution.py:19
  36.0 0.6 constant_dynamic-update-slice_fusion.10
  36.6 1.0 pad_maximum_fusion.7
  37.6 0.7 fusion.14
  38.4 0.7 collective-permute-done.8
  39.0 1.5 %collective-permute-start.13 = (bf16[128,1856]{1,0:T(8,128)(2,1)S(1)}, bf16[128,1856]{1,0:T(8,128)(2,1)S(1)}, u32[]{:S(2)}, u32[]{:S(2)}) collective-permute-start(bf16[128,1856]{1,0:T(8,128)(2,1)S(1)} %bitcast.138), channel_id=1, source_target_pairs={{0,96},{32,64},{64,32},{96,0},{1,97},{33,65},{65,33},{97,1},{2,98}... | collective-permute-start | bytes 1425416 | tf_op jit(solution)/shard_map/ppermute | solution.py:15
  40.5 1.8 %collective-permute-start.12 = (bf16[128,1856]{1,0:T(8,128)(2,1)S(1)}, bf16[128,1856]{1,0:T(8,128)(2,1)S(1)}, u32[]{:S(2)}, u32[]{:S(2)}) collective-permute-start(bf16[128,1856]{1,0:T(8,128)(2,1)S(1)} %bitcast.139), channel_id=1, source_target_pairs={{0,32},{32,0},{64,96},{96,64},{1,33},{33,1},{65,97},{97,65},{2,34}... | collective-permute-start | bytes 1425416 | tf_op jit(solution)/shard_map/ppermute | solution.py:15
  42.3 1.5 %add_convert_fusion.1 = bf16[256,2048]{1,0:T(8,128)(2,1)S(1)} fusion(f32[256,2048]{1,0:T(8,128)S(1)} %fusion.14, bf16[256,2048]{1,0:T(8,128)(2,1)} %collective-permute-done.8), kind=kLoop, calls=%fused_computation.4 | loop fusion | flops 1572864 | bytes 4194304 | tf_op jit(solution)/shard_map/convert_element_type | solution.py:103
  43.9 2.8 %collective-permute-start.11 = (bf16[64,2048]{1,0:T(8,128)(2,1)S(1)}, bf16[64,2048]{1,0:T(8,128)(2,1)S(1)}, u32[]{:S(2)}, u32[]{:S(2)}) collective-permute-start(bf16[64,2048]{1,0:T(8,128)(2,1)S(1)} %get-tuple-element.109), channel_id=1, source_target_pairs={{0,3},{1,2},{2,1},{3,0},{4,7},{5,6},{6,5},{7,4},{8,11},{9,10},{10,... | collective-permute-start | bytes 786440 | tf_op jit(solution)/shard_map/ppermute | solution.py:15
  46.7 0.9 collective-permute-start.10
  48.1 0.6 constant_dynamic-update-slice_fusion.9
  48.7 0.6 constant_dynamic-update-slice_fusion.8
  49.4 9.2 %collective-permute-done.11 = bf16[64,2048]{1,0:T(8,128)(2,1)S(1)} collective-permute-done((bf16[64,2048]{1,0:T(8,128)(2,1)S(1)}, bf16[64,2048]{1,0:T(8,128)(2,1)S(1)}, u32[]{:S(2)}, u32[]{:S(2)}) %collective-permute-start.11) | collective-permute-done | bytes 262176 | tf_op jit(solution)/shard_map/ppermute | solution.py:15
  58.6 0.6 collective-permute-done.9
  59.2 1.0 add_convert_fusion.2
  60.3 3.4 %all-to-all-start.1 = ((bf16[4,16,2048]{2,1,0:T(8,128)(2,1)}), bf16[4,16,2048]{2,1,0:T(8,128)(2,1)S(1)}, u32[]{:S(2)}, u32[]{:S(2)}) async-start(bf16[4,16,2048]{2,1,0:T(8,128)(2,1)} %bitcast.21), calls=%async_computation.1 | async-start | bytes 524288 | tf_op jit(solution)/shard_map/all_to_all | solution.py:33
  63.7 0.7 constant_dynamic-update-slice_fusion.7
  64.4 2.7 %collective-permute-start.15 = (bf16[64,2048]{1,0:T(8,128)(2,1)}, bf16[64,2048]{1,0:T(8,128)(2,1)S(1)}, u32[]{:S(2)}, u32[]{:S(2)}) collective-permute-start(bf16[64,2048]{1,0:T(8,128)(2,1)} %get-tuple-element.152), channel_id=1, source_target_pairs={{0,3},{1,2},{2,1},{3,0},{4,7},{5,6},{6,5},{7,4},{8,11},{9,10},{10,... | collective-permute-start | bytes 786440 | tf_op jit(solution)/shard_map/ppermute | solution.py:15
  67.3 5.2 %collective-permute-done.15 = bf16[64,2048]{1,0:T(8,128)(2,1)S(1)} collective-permute-done((bf16[64,2048]{1,0:T(8,128)(2,1)}, bf16[64,2048]{1,0:T(8,128)(2,1)S(1)}, u32[]{:S(2)}, u32[]{:S(2)}) %collective-permute-start.15) | collective-permute-done | bytes 262176 | tf_op jit(solution)/shard_map/ppermute | solution.py:15
  72.5 0.7 copy-done.4
  73.2 0.9 collective-permute-done.14
  74.2 0.7 broadcast_in_dim.12
  74.9 6.4 %all-to-all-start.2 = ((bf16[16,16,512]{2,1,0:T(8,128)(2,1)}), bf16[16,16,512]{2,1,0:T(8,128)(2,1)S(1)}, u32[]{:S(2)}, u32[]{:S(2)}) async-start(bf16[16,16,512]{2,1,0:T(8,128)(2,1)} %bitcast.24), calls=%async_computation.2 | async-start | bytes 524288 | tf_op jit(solution)/shard_map/all_to_all | solution.py:33
  81.7 3.4 %collective-permute-start.17 = (bf16[64,2048]{1,0:T(8,128)(2,1)}, bf16[64,2048]{1,0:T(8,128)(2,1)}, u32[]{:S(2)}, u32[]{:S(2)}) collective-permute-start(bf16[64,2048]{1,0:T(8,128)(2,1)} %get-tuple-element.152), channel_id=1, source_target_pairs={{0,2},{1,3},{2,0},{3,1},{4,6},{5,7},{6,4},{7,5},{8,10},{9,11},{10,... | collective-permute-start | bytes 786440 | tf_op jit(solution)/shard_map/ppermute | solution.py:15
  85.2 6.1 %collective-permute-done.17 = bf16[64,2048]{1,0:T(8,128)(2,1)} collective-permute-done((bf16[64,2048]{1,0:T(8,128)(2,1)}, bf16[64,2048]{1,0:T(8,128)(2,1)}, u32[]{:S(2)}, u32[]{:S(2)}) %collective-permute-start.17) | collective-permute-done | bytes 262176 | tf_op jit(solution)/shard_map/ppermute | solution.py:15
  91.3 2.1 %collective-permute-done.16 = bf16[128,1856]{1,0:T(8,128)(2,1)} collective-permute-done((bf16[128,1856]{1,0:T(8,128)(2,1)S(1)}, bf16[128,1856]{1,0:T(8,128)(2,1)}, u32[]{:S(2)}, u32[]{:S(2)}) %collective-permute-start.16) | collective-permute-done | bytes 475168 | tf_op jit(solution)/shard_map/ppermute | solution.py:15
  93.6 1.3 collective-permute-done.18
  95.6 1.3 copy-done.15
  97.0 1.3 convolution_convert_fusion.1
  98.8 0.7 copy-done.1
  99.5 1.0 constant_dynamic-update-slice_fusion.6
  100.4 1.0 constant_dynamic-update-slice_fusion.5
  101.4 1.4 %collective-permute-start.23 = (bf16[64,1856]{1,0:T(8,128)(2,1)S(1)}, bf16[64,1856]{1,0:T(8,128)(2,1)S(1)}, u32[]{:S(2)}, u32[]{:S(2)}) collective-permute-start(bf16[64,1856]{1,0:T(8,128)(2,1)S(1)} %get-tuple-element.104), channel_id=1, source_target_pairs={{0,64},{32,96},{64,0},{96,32},{1,65},{33,97},{65,1},{97,33},{2,66}... | collective-permute-start | bytes 712712 | tf_op jit(solution)/shard_map/ppermute | solution.py:15
  102.9 1.7 %collective-permute-start.22 = (bf16[64,1856]{1,0:T(8,128)(2,1)S(1)}, bf16[64,1856]{1,0:T(8,128)(2,1)S(1)}, u32[]{:S(2)}, u32[]{:S(2)}) collective-permute-start(bf16[64,1856]{1,0:T(8,128)(2,1)S(1)} %get-tuple-element.105), channel_id=1, source_target_pairs={{0,32},{32,0},{64,96},{96,64},{1,33},{33,1},{65,97},{97,65},{2,34}... | collective-permute-start | bytes 712712 | tf_op jit(solution)/shard_map/ppermute | solution.py:15
  104.6 2.9 %collective-permute-start.21 = (bf16[64,1856]{1,0:T(8,128)(2,1)S(1)}, bf16[64,1856]{1,0:T(8,128)(2,1)S(1)}, u32[]{:S(2)}, u32[]{:S(2)}) collective-permute-start(bf16[64,1856]{1,0:T(8,128)(2,1)S(1)} %get-tuple-element.106), channel_id=1, source_target_pairs={{0,3},{1,2},{2,1},{3,0},{4,7},{5,6},{6,5},{7,4},{8,11},{9,10},{10,... | collective-permute-start | bytes 712712 | tf_op jit(solution)/shard_map/ppermute | solution.py:15
  107.5 0.9 collective-permute-start.20
  108.3 3.3 %collective-permute-done.24 = bf16[64,1856]{1,0:T(8,128)(2,1)S(1)} collective-permute-done((bf16[64,1856]{1,0:T(8,128)(2,1)S(1)}, bf16[64,1856]{1,0:T(8,128)(2,1)S(1)}, u32[]{:S(2)}, u32[]{:S(2)}) %collective-permute-start.24) | collective-permute-done | bytes 237600 | tf_op jit(solution)/shard_map/ppermute | solution.py:15
  111.6 1.6 %collective-permute-start.19 = (bf16[64,1856]{1,0:T(8,128)(2,1)S(1)}, bf16[64,1856]{1,0:T(8,128)(2,1)S(1)}, u32[]{:S(2)}, u32[]{:S(2)}) collective-permute-start(bf16[64,1856]{1,0:T(8,128)(2,1)S(1)} %get-tuple-element.108), channel_id=1, source_target_pairs={{0,1},{1,0},{2,3},{3,2},{4,5},{5,4},{6,7},{7,6},{8,9},{9,8},{10,11... | collective-permute-start | bytes 712712 | tf_op jit(solution)/shard_map/ppermute | solution.py:15
  113.5 2.1 %collective-permute-done.22 = bf16[64,1856]{1,0:T(8,128)(2,1)S(1)} collective-permute-done((bf16[64,1856]{1,0:T(8,128)(2,1)S(1)}, bf16[64,1856]{1,0:T(8,128)(2,1)S(1)}, u32[]{:S(2)}, u32[]{:S(2)}) %collective-permute-start.22) | collective-permute-done | bytes 237600 | tf_op jit(solution)/shard_map/ppermute | solution.py:15
  115.6 2.6 %collective-permute-done.21 = bf16[64,1856]{1,0:T(8,128)(2,1)S(1)} collective-permute-done((bf16[64,1856]{1,0:T(8,128)(2,1)S(1)}, bf16[64,1856]{1,0:T(8,128)(2,1)S(1)}, u32[]{:S(2)}, u32[]{:S(2)}) %collective-permute-start.21) | collective-permute-done | bytes 237600 | tf_op jit(solution)/shard_map/ppermute | solution.py:15
  118.2 0.6 collective-permute-done.19
  119.1 2.9 %collective-permute-start.30 = (bf16[16,1856]{1,0:T(8,128)(2,1)S(1)}, bf16[16,1856]{1,0:T(8,128)(2,1)S(1)}, u32[]{:S(2)}, u32[]{:S(2)}) collective-permute-start(bf16[16,1856]{1,0:T(8,128)(2,1)S(1)} %get-tuple-element.141), channel_id=1, source_target_pairs={{0,3},{1,2},{2,1},{3,0},{4,7},{5,6},{6,5},{7,4},{8,11},{9,10},{10,... | collective-permute-start | bytes 178184 | tf_op jit(solution)/shard_map/ppermute | solution.py:15
  122.1 0.9 collective-permute-start.29
  123.3 1.4 collective-permute-start.27
  124.7 2.3 %collective-permute-start.26 = (bf16[16,1856]{1,0:T(8,128)(2,1)S(1)}, bf16[16,1856]{1,0:T(8,128)(2,1)S(1)}, u32[]{:S(2)}, u32[]{:S(2)}) collective-permute-start(bf16[16,1856]{1,0:T(8,128)(2,1)S(1)} %get-tuple-element.145), channel_id=1, source_target_pairs={{0,64},{32,96},{64,0},{96,32},{1,65},{33,97},{65,1},{97,33},{2,66}... | collective-permute-start | bytes 178184 | tf_op jit(solution)/shard_map/ppermute | solution.py:15
  127.0 0.8 collective-permute-done.29
  127.8 1.6 %collective-permute-start.25 = (bf16[16,1856]{1,0:T(8,128)(2,1)S(1)}, bf16[16,1856]{1,0:T(8,128)(2,1)S(1)}, u32[]{:S(2)}, u32[]{:S(2)}) collective-permute-start(bf16[16,1856]{1,0:T(8,128)(2,1)S(1)} %get-tuple-element.146), channel_id=1, source_target_pairs={{0,32},{32,0},{64,96},{96,64},{1,33},{33,1},{65,97},{97,65},{2,34}... | collective-permute-start | bytes 178184 | tf_op jit(solution)/shard_map/ppermute | solution.py:15
  129.4 3.5 %convolution_convert_fusion = bf16[512,1856]{0,1:T(8,128)(2,1)} fusion(bf16[512,512]{1,0:T(8,128)(2,1)S(1)} %bitcast.136, bf16[128,1856]{1,0:T(8,128)(2,1)S(1)} %copy-done.17, bf16[128,1856]{1,0:T(8,128)(2,1)} %collective-permute-done.16, bf16[128,1856]{1,0:T(8,128)(2,1)S(1)} %copy-done.19, bf16[128,1856]{1,0:T(8,128)(2,1)S(1)} %bitcast.141), kind=kOutput, calls=%fused_computation.1 | convolution fusion | flops 981630976 | bytes 4325376 | tf_op jit(solution)/shard_map/dot_general | solution.py:27
  132.9 6.3 %collective-permute-start.32 = (bf16[16,1856]{1,0:T(8,128)(2,1)S(1)}, bf16[16,1856]{1,0:T(8,128)(2,1)S(1)}, u32[]{:S(2)}, u32[]{:S(2)}) collective-permute-start(bf16[16,1856]{1,0:T(8,128)(2,1)S(1)} %add_convert_fusion.4), channel_id=1, source_target_pairs={{0,128},{128,0},{1,129},{129,1},{2,130},{130,2},{3,131},{131,3},{4... | collective-permute-start | bytes 178184 | tf_op jit(solution)/shard_map/ppermute | solution.py:15
  139.3 0.7 fusion.32
  139.9 1.9 %add_convert_fusion = bf16[464,2048]{1,0:T(8,128)(2,1)} fusion(f32[464,2048]{1,0:T(8,128)S(1)} %fusion.32, bf16[256,464]{1,0:T(8,128)(2,1)S(1)} %bitcast.135, bf16[256,2048]{1,0:T(8,128)(2,1)S(1)} %constant_dynamic-update-slice_fusion.4), kind=kOutput, calls=%fused_computation | convolution fusion | flops 488439808 | bytes 6987776 | tf_op jit(solution)/shard_map/dot_general | solution.py:27
  141.9 0.7 add_convert_fusion.3
  (104 shorter events, 5.1 us)
Async XLA Ops:
  0.6 33.7 %copy-start = (bf16[464,2048]{1,0:T(8,128)(2,1)S(1)}, bf16[464,2048]{1,0:T(8,128)(2,1)}, u32[]{:S(2)}) copy-start(bf16[464,2048]{1,0:T(8,128)(2,1)} %param.9) | copy-start | bytes 5701636
  0.6 22.8 %copy-start.13 = (bf16[16,1856]{1,0:T(8,128)(2,1)S(1)}, bf16[16,1856]{1,0:T(8,128)(2,1)}, u32[]{:S(2)}) copy-start(bf16[16,1856]{1,0:T(8,128)(2,1)} %param.5) | copy-start | bytes 178180
  0.7 19.7 %copy-start.12 = (bf16[16,2048]{1,0:T(8,128)(2,1)S(1)}, bf16[16,2048]{1,0:T(8,128)(2,1)}, u32[]{:S(2)}) copy-start(bf16[16,2048]{1,0:T(8,128)(2,1)} %param.6) | copy-start | bytes 196612
  0.7 10.2 %collective-permute-start = (bf16[16,1856]{1,0:T(8,128)(2,1)}, bf16[16,1856]{1,0:T(8,128)(2,1)S(1)}, u32[]{:S(2)}, u32[]{:S(2)}) collective-permute-start(bf16[16,1856]{1,0:T(8,128)(2,1)} %param.7), channel_id=1, source_target_pairs={{0,128},{128,0},{1,129},{129,1},{2,130},{130,2},{3,131},{131,3},{4... | collective-permute-start | bytes 178184 | tf_op jit(solution)/shard_map/ppermute | solution.py:15
  7.9 15.5 %collective-permute-start.1 = (bf16[16,1856]{1,0:T(8,128)(2,1)}, bf16[16,1856]{1,0:T(8,128)(2,1)S(1)}, u32[]{:S(2)}, u32[]{:S(2)}) collective-permute-start(bf16[16,1856]{1,0:T(8,128)(2,1)} %param.5), channel_id=1, source_target_pairs={{0,128},{128,0},{1,129},{129,1},{2,130},{130,2},{3,131},{131,3},{4... | collective-permute-start | bytes 178184 | tf_op jit(solution)/shard_map/ppermute | solution.py:15
  13.0 20.6 %all-to-all-start = ((bf16[16,32,464]{2,1,0:T(8,128)(2,1)}), bf16[16,32,464]{2,1,0:T(8,128)(2,1)S(1)}, u32[]{:S(2)}, u32[]{:S(2)}) async-start(bf16[16,32,464]{2,1,0:T(8,128)(2,1)} %bitcast.1), calls=%async_computation | async-start | bytes 1048576 | tf_op jit(solution)/shard_map/all_to_all | solution.py:33
  20.4 8.8 %collective-permute-start.7 = (bf16[16,2048]{1,0:T(8,128)(2,1)S(1)}, bf16[16,2048]{1,0:T(8,128)(2,1)S(1)}, u32[]{:S(2)}, u32[]{:S(2)}) collective-permute-start(bf16[16,2048]{1,0:T(8,128)(2,1)S(1)} %get-tuple-element.52), channel_id=1, source_target_pairs={{0,24},{8,16},{16,8},{24,0},{1,25},{9,17},{17,9},{25,1},{2,26},{10... | collective-permute-start | bytes 196616 | tf_op jit(solution)/shard_map/ppermute | solution.py:15
  23.4 10.1 %collective-permute-start.4 = (bf16[2,16,1856]{2,1,0:T(8,128)(2,1)S(1)}, bf16[2,16,1856]{2,1,0:T(8,128)(2,1)S(1)}, u32[]{:S(2)}, u32[]{:S(2)}) collective-permute-start(bf16[2,16,1856]{2,1,0:T(8,128)(2,1)S(1)} %get-tuple-element.148), channel_id=1, source_target_pairs={{0,3},{1,2},{2,1},{3,0},{4,7},{5,6},{6,5},{7,4},{8,11},{9,10},{10,... | collective-permute-start | bytes 356360 | tf_op jit(solution)/shard_map/ppermute | solution.py:15
  26.2 7.3 %collective-permute-start.3 = (bf16[2,16,1856]{2,1,0:T(8,128)(2,1)S(1)}, bf16[2,16,1856]{2,1,0:T(8,128)(2,1)S(1)}, u32[]{:S(2)}, u32[]{:S(2)}) collective-permute-start(bf16[2,16,1856]{2,1,0:T(8,128)(2,1)S(1)} %get-tuple-element.148), channel_id=1, source_target_pairs={{0,2},{1,3},{2,0},{3,1},{4,6},{5,7},{6,4},{7,5},{8,10},{9,11},{10,... | collective-permute-start | bytes 356360 | tf_op jit(solution)/shard_map/ppermute | solution.py:15
  27.1 6.5 %collective-permute-start.2 = (bf16[2,16,1856]{2,1,0:T(8,128)(2,1)S(1)}, bf16[2,16,1856]{2,1,0:T(8,128)(2,1)}, u32[]{:S(2)}, u32[]{:S(2)}) collective-permute-start(bf16[2,16,1856]{2,1,0:T(8,128)(2,1)S(1)} %get-tuple-element.148), channel_id=1, source_target_pairs={{0,1},{1,0},{2,3},{3,2},{4,5},{5,4},{6,7},{7,6},{8,9},{9,8},{10,11... | collective-permute-start | bytes 356360 | tf_op jit(solution)/shard_map/ppermute | solution.py:15
  27.6 5.2 %collective-permute-start.6 = (bf16[16,2048]{1,0:T(8,128)(2,1)S(1)}, bf16[16,2048]{1,0:T(8,128)(2,1)S(1)}, u32[]{:S(2)}, u32[]{:S(2)}) collective-permute-start(bf16[16,2048]{1,0:T(8,128)(2,1)S(1)} %get-tuple-element.52), channel_id=1, source_target_pairs={{0,16},{8,24},{16,0},{24,8},{1,17},{9,25},{17,1},{25,9},{2,18},{10... | collective-permute-start | bytes 196616 | tf_op jit(solution)/shard_map/ppermute | solution.py:15
  29.2 4.3 %copy-start.6 = (bf16[16,2048]{1,0:T(8,128)(2,1)}, bf16[16,2048]{1,0:T(8,128)(2,1)S(1)}, u32[]{:S(2)}) copy-start(bf16[16,2048]{1,0:T(8,128)(2,1)S(1)} %collective-permute-done.7) | copy-start | bytes 196612
  29.2 4.3 %collective-permute-start.5 = (bf16[16,2048]{1,0:T(8,128)(2,1)S(1)}, bf16[16,2048]{1,0:T(8,128)(2,1)S(1)}, u32[]{:S(2)}, u32[]{:S(2)}) collective-permute-start(bf16[16,2048]{1,0:T(8,128)(2,1)S(1)} %get-tuple-element.52), channel_id=1, source_target_pairs={{0,8},{8,0},{16,24},{24,16},{1,9},{9,1},{17,25},{25,17},{2,10},{10... | collective-permute-start | bytes 196616 | tf_op jit(solution)/shard_map/ppermute | solution.py:15
  32.8 0.8 copy-start.8
  33.5 0.6 copy-start.10
  36.0 3.0 %collective-permute-start.8 = (bf16[256,2048]{1,0:T(8,128)(2,1)}, bf16[256,2048]{1,0:T(8,128)(2,1)}, u32[]{:S(2)}, u32[]{:S(2)}) collective-permute-start(bf16[256,2048]{1,0:T(8,128)(2,1)} %convolution_convert_fusion.2), channel_id=1, source_target_pairs={{0,4},{4,0},{1,5},{5,1},{2,6},{6,2},{3,7},{7,3},{8,12},{12,8},{9,1... | collective-permute-start | bytes 3145736 | tf_op jit(solution)/shard_map/ppermute | solution.py:15
  37.6 2.9 %copy-start.2 = (bf16[4,2,16,1856]{3,2,1,0:T(8,128)(2,1)}, bf16[4,2,16,1856]{3,2,1,0:T(8,128)(2,1)S(1)}, u32[]{:S(2)}) copy-start(bf16[4,2,16,1856]{3,2,1,0:T(8,128)(2,1)S(1)} %pad_maximum_fusion.7) | copy-start | bytes 1425412
  39.0 9.1 %copy-start.11 = (bf16[16,2048]{1,0:T(8,128)(2,1)S(1)}, bf16[16,2048]{1,0:T(8,128)(2,1)}, u32[]{:S(2)}) copy-start(bf16[16,2048]{1,0:T(8,128)(2,1)} %copy-done.10) | copy-start | bytes 196612
  39.0 9.7 %copy-start.9 = (bf16[16,2048]{1,0:T(8,128)(2,1)S(1)}, bf16[16,2048]{1,0:T(8,128)(2,1)}, u32[]{:S(2)}) copy-start(bf16[16,2048]{1,0:T(8,128)(2,1)} %copy-done.8) | copy-start | bytes 196612
  39.0 20.2 %collective-permute-start.13 = (bf16[128,1856]{1,0:T(8,128)(2,1)S(1)}, bf16[128,1856]{1,0:T(8,128)(2,1)S(1)}, u32[]{:S(2)}, u32[]{:S(2)}) collective-permute-start(bf16[128,1856]{1,0:T(8,128)(2,1)S(1)} %bitcast.138), channel_id=1, source_target_pairs={{0,96},{32,64},{64,32},{96,0},{1,97},{33,65},{65,33},{97,1},{2,98}... | collective-permute-start | bytes 1425416 | tf_op jit(solution)/shard_map/ppermute | solution.py:15
  40.5 18.8 %collective-permute-start.12 = (bf16[128,1856]{1,0:T(8,128)(2,1)S(1)}, bf16[128,1856]{1,0:T(8,128)(2,1)S(1)}, u32[]{:S(2)}, u32[]{:S(2)}) collective-permute-start(bf16[128,1856]{1,0:T(8,128)(2,1)S(1)} %bitcast.139), channel_id=1, source_target_pairs={{0,32},{32,0},{64,96},{96,64},{1,33},{33,1},{65,97},{97,65},{2,34}... | collective-permute-start | bytes 1425416 | tf_op jit(solution)/shard_map/ppermute | solution.py:15
  43.8 19.9 %copy-start.7 = (bf16[16,2048]{1,0:T(8,128)(2,1)S(1)}, bf16[16,2048]{1,0:T(8,128)(2,1)}, u32[]{:S(2)}) copy-start(bf16[16,2048]{1,0:T(8,128)(2,1)} %copy-done.6) | copy-start | bytes 196612
  43.9 14.7 %collective-permute-start.11 = (bf16[64,2048]{1,0:T(8,128)(2,1)S(1)}, bf16[64,2048]{1,0:T(8,128)(2,1)S(1)}, u32[]{:S(2)}, u32[]{:S(2)}) collective-permute-start(bf16[64,2048]{1,0:T(8,128)(2,1)S(1)} %get-tuple-element.109), channel_id=1, source_target_pairs={{0,3},{1,2},{2,1},{3,0},{4,7},{5,6},{6,5},{7,4},{8,11},{9,10},{10,... | collective-permute-start | bytes 786440 | tf_op jit(solution)/shard_map/ppermute | solution.py:15
  46.7 11.9 %collective-permute-start.10 = (bf16[64,2048]{1,0:T(8,128)(2,1)S(1)}, bf16[64,2048]{1,0:T(8,128)(2,1)S(1)}, u32[]{:S(2)}, u32[]{:S(2)}) collective-permute-start(bf16[64,2048]{1,0:T(8,128)(2,1)S(1)} %get-tuple-element.110), channel_id=1, source_target_pairs={{0,2},{1,3},{2,0},{3,1},{4,6},{5,7},{6,4},{7,5},{8,10},{9,11},{10,... | collective-permute-start | bytes 786440 | tf_op jit(solution)/shard_map/ppermute | solution.py:15
  47.5 11.7 %collective-permute-start.9 = (bf16[64,2048]{1,0:T(8,128)(2,1)S(1)}, bf16[64,2048]{1,0:T(8,128)(2,1)S(1)}, u32[]{:S(2)}, u32[]{:S(2)}) collective-permute-start(bf16[64,2048]{1,0:T(8,128)(2,1)S(1)} %get-tuple-element.111), channel_id=1, source_target_pairs={{0,1},{1,0},{2,3},{3,2},{4,5},{5,4},{6,7},{7,6},{8,9},{9,8},{10,11... | collective-permute-start | bytes 786440 | tf_op jit(solution)/shard_map/ppermute | solution.py:15
  49.4 10.9 %copy-start.14 = (bf16[64,2048]{1,0:T(8,128)(2,1)}, bf16[64,2048]{1,0:T(8,128)(2,1)S(1)}, u32[]{:S(2)}) copy-start(bf16[64,2048]{1,0:T(8,128)(2,1)S(1)} %get-tuple-element.154) | copy-start | bytes 786436
  49.4 32.0 %copy-start.3 = (bf16[4,2,16,1856]{3,2,1,0:T(8,128)(2,1)S(1)}, bf16[4,2,16,1856]{3,2,1,0:T(8,128)(2,1)}, u32[]{:S(2)}) copy-start(bf16[4,2,16,1856]{3,2,1,0:T(8,128)(2,1)} %copy-done.2) | copy-start | bytes 1425412
  59.2 1.0 copy-start.16
  59.2 1.1 copy-start.18
  60.3 13.8 %all-to-all-start.1 = ((bf16[4,16,2048]{2,1,0:T(8,128)(2,1)}), bf16[4,16,2048]{2,1,0:T(8,128)(2,1)S(1)}, u32[]{:S(2)}, u32[]{:S(2)}) async-start(bf16[4,16,2048]{2,1,0:T(8,128)(2,1)} %bitcast.21), calls=%async_computation.1 | async-start | bytes 524288 | tf_op jit(solution)/shard_map/all_to_all | solution.py:33
  64.4 8.1 %collective-permute-start.15 = (bf16[64,2048]{1,0:T(8,128)(2,1)}, bf16[64,2048]{1,0:T(8,128)(2,1)S(1)}, u32[]{:S(2)}, u32[]{:S(2)}) collective-permute-start(bf16[64,2048]{1,0:T(8,128)(2,1)} %get-tuple-element.152), channel_id=1, source_target_pairs={{0,3},{1,2},{2,1},{3,0},{4,7},{5,6},{6,5},{7,4},{8,11},{9,10},{10,... | collective-permute-start | bytes 786440 | tf_op jit(solution)/shard_map/ppermute | solution.py:15
  67.0 7.0 %collective-permute-start.14 = (bf16[64,2048]{1,0:T(8,128)(2,1)}, bf16[64,2048]{1,0:T(8,128)(2,1)}, u32[]{:S(2)}, u32[]{:S(2)}) collective-permute-start(bf16[64,2048]{1,0:T(8,128)(2,1)} %get-tuple-element.152), channel_id=1, source_target_pairs={{0,1},{1,0},{2,3},{3,2},{4,5},{5,4},{6,7},{7,6},{8,9},{9,8},{10,11... | collective-permute-start | bytes 786440 | tf_op jit(solution)/shard_map/ppermute | solution.py:15
  72.5 0.7 copy-start.4
  74.9 18.5 %all-to-all-start.2 = ((bf16[16,16,512]{2,1,0:T(8,128)(2,1)}), bf16[16,16,512]{2,1,0:T(8,128)(2,1)S(1)}, u32[]{:S(2)}, u32[]{:S(2)}) async-start(bf16[16,16,512]{2,1,0:T(8,128)(2,1)} %bitcast.24), calls=%async_computation.2 | async-start | bytes 524288 | tf_op jit(solution)/shard_map/all_to_all | solution.py:33
  81.3 12.1 %collective-permute-start.16 = (bf16[128,1856]{1,0:T(8,128)(2,1)S(1)}, bf16[128,1856]{1,0:T(8,128)(2,1)}, u32[]{:S(2)}, u32[]{:S(2)}) collective-permute-start(bf16[128,1856]{1,0:T(8,128)(2,1)S(1)} %bitcast.140), channel_id=1, source_target_pairs={{0,64},{32,96},{64,0},{96,32},{1,65},{33,97},{65,1},{97,33},{2,66}... | collective-permute-start | bytes 1425416 | tf_op jit(solution)/shard_map/ppermute | solution.py:15
  81.7 9.7 %collective-permute-start.17 = (bf16[64,2048]{1,0:T(8,128)(2,1)}, bf16[64,2048]{1,0:T(8,128)(2,1)}, u32[]{:S(2)}, u32[]{:S(2)}) collective-permute-start(bf16[64,2048]{1,0:T(8,128)(2,1)} %get-tuple-element.152), channel_id=1, source_target_pairs={{0,2},{1,3},{2,0},{3,1},{4,6},{5,7},{6,4},{7,5},{8,10},{9,11},{10,... | collective-permute-start | bytes 786440 | tf_op jit(solution)/shard_map/ppermute | solution.py:15
  93.5 1.5 %collective-permute-start.18 = (bf16[16,16,512]{2,1,0:T(8,128)(2,1)S(1)}, bf16[16,16,512]{2,1,0:T(8,128)(2,1)S(1)}, u32[]{:S(2)}, u32[]{:S(2)}) collective-permute-start(bf16[16,16,512]{2,1,0:T(8,128)(2,1)S(1)} %all-to-all-done.2), channel_id=1, source_target_pairs={{0,4},{4,0},{1,5},{5,1},{2,6},{6,2},{3,7},{7,3},{8,12},{12,8},{9,1... | collective-permute-start | bytes 786440 | tf_op jit(solution)/shard_map/ppermute | solution.py:15
  95.4 1.5 %copy-start.15 = (bf16[512,1856]{0,1:T(8,128)(2,1)S(1)}, bf16[512,1856]{0,1:T(8,128)(2,1)}, u32[]{:S(2)}) copy-start(bf16[512,1856]{0,1:T(8,128)(2,1)} %param.8) | copy-start | bytes 5701636
  98.2 1.2 copy-start.1
  98.3 15.0 %copy-start.5 = (bf16[64,2048]{1,0:T(8,128)(2,1)S(1)}, bf16[64,2048]{1,0:T(8,128)(2,1)}, u32[]{:S(2)}) copy-start(bf16[64,2048]{1,0:T(8,128)(2,1)} %copy-done.4) | copy-start | bytes 786436
  98.4 13.2 %collective-permute-start.24 = (bf16[64,1856]{1,0:T(8,128)(2,1)S(1)}, bf16[64,1856]{1,0:T(8,128)(2,1)S(1)}, u32[]{:S(2)}, u32[]{:S(2)}) collective-permute-start(bf16[64,1856]{1,0:T(8,128)(2,1)S(1)} %get-tuple-element.103), channel_id=1, source_target_pairs={{0,96},{32,64},{64,32},{96,0},{1,97},{33,65},{65,33},{97,1},{2,98}... | collective-permute-start | bytes 712712 | tf_op jit(solution)/shard_map/ppermute | solution.py:15
  101.4 12.0 %collective-permute-start.23 = (bf16[64,1856]{1,0:T(8,128)(2,1)S(1)}, bf16[64,1856]{1,0:T(8,128)(2,1)S(1)}, u32[]{:S(2)}, u32[]{:S(2)}) collective-permute-start(bf16[64,1856]{1,0:T(8,128)(2,1)S(1)} %get-tuple-element.104), channel_id=1, source_target_pairs={{0,64},{32,96},{64,0},{96,32},{1,65},{33,97},{65,1},{97,33},{2,66}... | collective-permute-start | bytes 712712 | tf_op jit(solution)/shard_map/ppermute | solution.py:15
  102.9 12.7 %collective-permute-start.22 = (bf16[64,1856]{1,0:T(8,128)(2,1)S(1)}, bf16[64,1856]{1,0:T(8,128)(2,1)S(1)}, u32[]{:S(2)}, u32[]{:S(2)}) collective-permute-start(bf16[64,1856]{1,0:T(8,128)(2,1)S(1)} %get-tuple-element.105), channel_id=1, source_target_pairs={{0,32},{32,0},{64,96},{96,64},{1,33},{33,1},{65,97},{97,65},{2,34}... | collective-permute-start | bytes 712712 | tf_op jit(solution)/shard_map/ppermute | solution.py:15
  104.6 13.6 %collective-permute-start.21 = (bf16[64,1856]{1,0:T(8,128)(2,1)S(1)}, bf16[64,1856]{1,0:T(8,128)(2,1)S(1)}, u32[]{:S(2)}, u32[]{:S(2)}) collective-permute-start(bf16[64,1856]{1,0:T(8,128)(2,1)S(1)} %get-tuple-element.106), channel_id=1, source_target_pairs={{0,3},{1,2},{2,1},{3,0},{4,7},{5,6},{6,5},{7,4},{8,11},{9,10},{10,... | collective-permute-start | bytes 712712 | tf_op jit(solution)/shard_map/ppermute | solution.py:15
  107.5 10.8 %collective-permute-start.20 = (bf16[64,1856]{1,0:T(8,128)(2,1)S(1)}, bf16[64,1856]{1,0:T(8,128)(2,1)S(1)}, u32[]{:S(2)}, u32[]{:S(2)}) collective-permute-start(bf16[64,1856]{1,0:T(8,128)(2,1)S(1)} %get-tuple-element.107), channel_id=1, source_target_pairs={{0,2},{1,3},{2,0},{3,1},{4,6},{5,7},{6,4},{7,5},{8,10},{9,11},{10,... | collective-permute-start | bytes 712712 | tf_op jit(solution)/shard_map/ppermute | solution.py:15
  111.6 7.2 %collective-permute-start.19 = (bf16[64,1856]{1,0:T(8,128)(2,1)S(1)}, bf16[64,1856]{1,0:T(8,128)(2,1)S(1)}, u32[]{:S(2)}, u32[]{:S(2)}) collective-permute-start(bf16[64,1856]{1,0:T(8,128)(2,1)S(1)} %get-tuple-element.108), channel_id=1, source_target_pairs={{0,1},{1,0},{2,3},{3,2},{4,5},{5,4},{6,7},{7,6},{8,9},{9,8},{10,11... | collective-permute-start | bytes 712712 | tf_op jit(solution)/shard_map/ppermute | solution.py:15
  113.3 16.0 %copy-start.17 = (bf16[128,1856]{1,0:T(8,128)(2,1)S(1)}, bf16[128,1856]{1,0:T(8,128)(2,1)}, u32[]{:S(2)}) copy-start(bf16[128,1856]{1,0:T(8,128)(2,1)} %copy-done.16) | copy-start | bytes 1425412
  113.4 16.0 %copy-start.19 = (bf16[128,1856]{1,0:T(8,128)(2,1)S(1)}, bf16[128,1856]{1,0:T(8,128)(2,1)}, u32[]{:S(2)}) copy-start(bf16[128,1856]{1,0:T(8,128)(2,1)} %copy-done.18) | copy-start | bytes 1425412
  113.4 19.5 %collective-permute-start.31 = (bf16[256,2048]{1,0:T(8,128)(2,1)S(1)}, bf16[256,2048]{1,0:T(8,128)(2,1)S(1)}, u32[]{:S(2)}, u32[]{:S(2)}) collective-permute-start(bf16[256,2048]{1,0:T(8,128)(2,1)S(1)} %constant_dynamic-update-slice_fusion.4), channel_id=1, source_target_pairs={{0,4},{4,0},{1,5},{5,1},{2,6},{6,2},{3,7},{7,3},{8,12},{12,8},{9,1... | collective-permute-start | bytes 3145736 | tf_op jit(solution)/shard_map/ppermute | solution.py:15
  119.1 5.6 %collective-permute-start.30 = (bf16[16,1856]{1,0:T(8,128)(2,1)S(1)}, bf16[16,1856]{1,0:T(8,128)(2,1)S(1)}, u32[]{:S(2)}, u32[]{:S(2)}) collective-permute-start(bf16[16,1856]{1,0:T(8,128)(2,1)S(1)} %get-tuple-element.141), channel_id=1, source_target_pairs={{0,3},{1,2},{2,1},{3,0},{4,7},{5,6},{6,5},{7,4},{8,11},{9,10},{10,... | collective-permute-start | bytes 178184 | tf_op jit(solution)/shard_map/ppermute | solution.py:15
  122.1 5.7 %collective-permute-start.29 = (bf16[16,1856]{1,0:T(8,128)(2,1)S(1)}, bf16[16,1856]{1,0:T(8,128)(2,1)S(1)}, u32[]{:S(2)}, u32[]{:S(2)}) collective-permute-start(bf16[16,1856]{1,0:T(8,128)(2,1)S(1)} %get-tuple-element.142), channel_id=1, source_target_pairs={{0,2},{1,3},{2,0},{3,1},{4,6},{5,7},{6,4},{7,5},{8,10},{9,11},{10,... | collective-permute-start | bytes 178184 | tf_op jit(solution)/shard_map/ppermute | solution.py:15
  122.9 9.9 %collective-permute-start.28 = (bf16[16,1856]{1,0:T(8,128)(2,1)S(1)}, bf16[16,1856]{1,0:T(8,128)(2,1)S(1)}, u32[]{:S(2)}, u32[]{:S(2)}) collective-permute-start(bf16[16,1856]{1,0:T(8,128)(2,1)S(1)} %get-tuple-element.143), channel_id=1, source_target_pairs={{0,1},{1,0},{2,3},{3,2},{4,5},{5,4},{6,7},{7,6},{8,9},{9,8},{10,11... | collective-permute-start | bytes 178184 | tf_op jit(solution)/shard_map/ppermute | solution.py:15
  123.3 9.5 %collective-permute-start.27 = (bf16[16,1856]{1,0:T(8,128)(2,1)S(1)}, bf16[16,1856]{1,0:T(8,128)(2,1)S(1)}, u32[]{:S(2)}, u32[]{:S(2)}) collective-permute-start(bf16[16,1856]{1,0:T(8,128)(2,1)S(1)} %get-tuple-element.144), channel_id=1, source_target_pairs={{0,96},{32,64},{64,32},{96,0},{1,97},{33,65},{65,33},{97,1},{2,98}... | collective-permute-start | bytes 178184 | tf_op jit(solution)/shard_map/ppermute | solution.py:15
  124.7 8.2 %collective-permute-start.26 = (bf16[16,1856]{1,0:T(8,128)(2,1)S(1)}, bf16[16,1856]{1,0:T(8,128)(2,1)S(1)}, u32[]{:S(2)}, u32[]{:S(2)}) collective-permute-start(bf16[16,1856]{1,0:T(8,128)(2,1)S(1)} %get-tuple-element.145), channel_id=1, source_target_pairs={{0,64},{32,96},{64,0},{96,32},{1,65},{33,97},{65,1},{97,33},{2,66}... | collective-permute-start | bytes 178184 | tf_op jit(solution)/shard_map/ppermute | solution.py:15
  127.8 5.1 %collective-permute-start.25 = (bf16[16,1856]{1,0:T(8,128)(2,1)S(1)}, bf16[16,1856]{1,0:T(8,128)(2,1)S(1)}, u32[]{:S(2)}, u32[]{:S(2)}) collective-permute-start(bf16[16,1856]{1,0:T(8,128)(2,1)S(1)} %get-tuple-element.146), channel_id=1, source_target_pairs={{0,32},{32,0},{64,96},{96,64},{1,33},{33,1},{65,97},{97,65},{2,34}... | collective-permute-start | bytes 178184 | tf_op jit(solution)/shard_map/ppermute | solution.py:15
  132.9 9.0 %collective-permute-start.32 = (bf16[16,1856]{1,0:T(8,128)(2,1)S(1)}, bf16[16,1856]{1,0:T(8,128)(2,1)S(1)}, u32[]{:S(2)}, u32[]{:S(2)}) collective-permute-start(bf16[16,1856]{1,0:T(8,128)(2,1)S(1)} %add_convert_fusion.4), channel_id=1, source_target_pairs={{0,128},{128,0},{1,129},{129,1},{2,130},{130,2},{3,131},{131,3},{4... | collective-permute-start | bytes 178184 | tf_op jit(solution)/shard_map/ppermute | solution.py:15
